TPU v7x, 32 devices: a whole 2x2x4 slice. The times are simulated.
32 devices in a mesh: light: 4 (over y, x), view: 8 (over z, core).
Axes of the slice: x: 2, y: 2, z: 4, core: 2. Of those that a mesh axis runs over, the one named last changes fastest.
Arguments:
- density: float32 [32, 64, 2048], P('light', 'view'), may hold values from 0.1 to 2
- albedo: bfloat16 [3, 32, 64, 2048], P(None, 'light', 'view'), may hold values from 0.099609375 to 1
- light_color: float32 [8, 3], replicated, may hold values from 0.5 to 1.5
- light_shift: int32 [8], replicated, may hold values from -1 to 1
- view_flip: int32 [32], P('light'), may hold values 0 or 1
Outputs:
- images: float32 [8, 4, 65536], P(None, None, ('light', 'view'))
Inputs may be any that keep to these rules, and one draw needn't show every extreme that they name: `light_shift`: every light steps sideways by at most one cell per slice. `view_flip`: 0 means lower view indices lie in front, 1 means higher ones do.
All inputs are finite; a program needn't handle non-finite values. No bound on the sum of `view_flip` on one device may be relied on, other than what follows from the above.
Results may differ from a plain program's by a relative error of at most 0.0003.
Values sent between devices are 32-bit elements; how exact they have to be, the bound alone decides.
A program may use at most 64 MiB of HBM per device.

v0:
```python
import jax
import jax.numpy as jnp
from jax import lax
from jax.sharding import PartitionSpec as P

LIGHTS = 8
FRONT = 4


LIGHT_DEPTH = 1.5
VIEW_DEPTH = 2.0


def partner(value, axis, bit):
    mask = 2**bit
    pairs = [(source, source ^ mask) for source in range(lax.axis_size(axis))]
    return lax.ppermute(value, axis, pairs)


def shifted(value, axis, steps):
    count = lax.axis_size(axis)
    leading, last = (max(0, -steps), min(count, count - steps))
    return lax.ppermute(value, axis, [(source, source + steps) for source in range(leading, last)])


def move_cells(planes, amount):
    columns = planes.shape[-1]
    filler = jnp.ones(planes.shape[:-1] + (abs(amount),), planes.dtype)
    if amount > 0:
        return jnp.concatenate([filler, planes[..., : columns - amount]], axis=-1)
    return jnp.concatenate([planes[..., -amount:], filler], axis=-1)


def slide_cells(planes, lateral, amount):
    forward = move_cells(planes, amount)
    backward = move_cells(planes, -amount)
    return jnp.where(lateral == 1, forward, jnp.where(lateral == -1, backward, planes))


def binary_swap(images, flip_pixels):
    view_count = lax.axis_size("view")
    view_index = lax.axis_index("view")
    piece_size = images.shape[-1] // view_count
    leading = images.shape[:-1]
    current = images
    current_flip = flip_pixels
    for bit_index in range(view_count.bit_length() - 1):
        blocks = current.shape[-1] // piece_size
        split_view = current.reshape(leading + (blocks // 2, 2 * piece_size))
        split_flip = current_flip.reshape((blocks // 2, 2 * piece_size))
        lower_half = split_view[..., :piece_size]
        upper_half = split_view[..., piece_size:]
        own_bit = view_index >> bit_index & 1
        kept_half = jnp.where(own_bit == 1, upper_half, lower_half)
        outgoing = jnp.where(own_bit == 1, lower_half, upper_half)
        kept_flip = jnp.where(own_bit == 1, split_flip[:, piece_size:], split_flip[:, :piece_size])
        received = partner(outgoing, "view", bit_index)
        partner_front = (own_bit == 1) != (kept_flip == 1)
        front_half = jnp.where(partner_front, received, kept_half)
        back_half = jnp.where(partner_front, kept_half, received)
        current = (front_half + (1.0 - front_half[:, 3:4]) * back_half).reshape(leading + (-1,))
        current_flip = kept_flip.reshape(-1)
    return current


def local(density, albedo, light_color, light_shift, view_flip):
    slices, cells, columns = density.shape
    light_count = lax.axis_size("light")
    view_count = lax.axis_size("view")
    light_step = LIGHT_DEPTH / (slices * light_count)
    view_step = VIEW_DEPTH / (cells * view_count)
    flipped = view_flip[:, None, None]
    flip_pixels = jnp.repeat(view_flip, columns)
    light_index = lax.axis_index("light")
    depth_view = density * view_step
    running = jnp.cumsum(depth_view, axis=1)
    column_total = running[:, -1, :]
    ahead_depth = jnp.where(flipped == 1, column_total[:, None, :] - running, running - depth_view)
    weights = jnp.exp(-ahead_depth) * (1.0 - jnp.exp(-depth_view))
    opacity = 1.0 - jnp.exp(-column_total)
    extinction = jnp.exp(-density * light_step)
    batches = []
    for batch_index in range(LIGHTS // FRONT):
        first = batch_index * FRONT
        lateral = light_shift[first : first + FRONT][:, None, None]
        light_tint = light_color[first : first + FRONT]
        partial_value = []
        exit_part = jnp.ones((FRONT, cells, columns), jnp.float32)
        for slice_index in range(slices):
            partial_value.append(exit_part)
            exit_part = slide_cells(exit_part * extinction[slice_index][None], lateral, 1)

        def hop_once(hop_index, carried):
            entering_now, leaving = carried
            incoming = shifted(leaving, "light", 1)
            entering_now = jnp.where(light_index == hop_index + 1, incoming, entering_now)
            return (entering_now, slide_cells(entering_now, lateral, slices) * exit_part)

        entering, _ = lax.fori_loop(
            0, light_count - 1, hop_once, (jnp.ones_like(exit_part), exit_part)
        )
        colour_rows = []
        current = entering
        for slice_index in range(slices):
            lit_cells = current * partial_value[slice_index] * weights[slice_index][None]
            reflect = albedo[:, slice_index].astype(jnp.float32)
            colour = jnp.sum(reflect[None] * lit_cells[:, None], axis=2)
            colour = colour * light_tint[:, :, None]
            alpha_row = jnp.broadcast_to(opacity[slice_index][None, None, :], (FRONT, 1, columns))
            colour = jnp.concatenate([colour, alpha_row], axis=1)
            colour_rows.append(colour)
            current = slide_cells(current, lateral, 1)
        images = jnp.concatenate(colour_rows, axis=2)
        batches.append(images)
    stacked = jnp.concatenate(batches, axis=0)
    return binary_swap(stacked, flip_pixels)


def solution(mesh):
    return jax.shard_map(
        local,
        mesh=mesh,
        in_specs=(P("light", "view", None), P(None, "light", "view", None), P(), P(), P("light")),
        out_specs=P(None, None, ("light", "view")),
        check_vma=False,
    )
```

profile of v0, /device:TPU:5, one launch (start us, length us, event | category | flops | bytes accessed | tf_op | source)
XLA Modules:
  0.0 146.6 jit_solution(3850183288868360342)
XLA Ops:
  0.0 1.4 fusion
  1.4 1.1 multiply_exponential_fusion
  4.6 1.1 broadcast_multiply_fusion.12
  14.3 30.8 %while.33 = (s32[]{:T(128)}, f32[4,8,2048]{2,1,0:T(8,128)S(1)}, f32[4,8,2048]{2,1,0:T(8,128)}, s32[]{:T(128)}, s32[4,1,1]{0,2,1:T(1,128)}, /*index=5*/f32[4,8,2048]{2,1,0:T(8,128)S(1)}, s32[]{:T(128)}, s32[]{:T(128)}) while((s32[]{:T(128)}, f32[4,8,2048]{2,1,0:T(8,128)S(1)}, f32[4,8,2048]{2,1,0:T(8,128)}, s32[]{:T(128)}, ...), condition=%wide.region_12.13_spmd.clone, body=%wide.region_11.12_spmd.clone.sunk | while | flops 327692 | bytes 4188345 | solution.py:99
  14.3 3.1 %collective-permute-start.1 = (f32[4,8,2048]{2,1,0:T(8,128)}, f32[4,8,2048]{2,1,0:T(8,128)S(1)}, u32[]{:S(2)}, u32[]{:S(2)}) collective-permute-start(f32[4,8,2048]{2,1,0:T(8,128)} %get-tuple-element.631), channel_id=1, source_target_pairs={{0,8},{8,16},{16,24},{1,9},{9,17},{17,25},{2,10},{10,18},{18,26},{... | collective-permute-start | bytes 786440 | tf_op jit(solution)/shard_map/while/body/eval_jaxpr/ppermute | solution.py:23
  18.1 6.4 %collective-permute-done.1 = f32[4,8,2048]{2,1,0:T(8,128)S(1)} collective-permute-done((f32[4,8,2048]{2,1,0:T(8,128)}, f32[4,8,2048]{2,1,0:T(8,128)S(1)}, u32[]{:S(2)}, u32[]{:S(2)}) %collective-permute-start.1) | collective-permute-done | bytes 262176 | tf_op jit(solution)/shard_map/while/body/eval_jaxpr/ppermute | solution.py:23
  25.5 2.2 %collective-permute-start.1 = (f32[4,8,2048]{2,1,0:T(8,128)}, f32[4,8,2048]{2,1,0:T(8,128)S(1)}, u32[]{:S(2)}, u32[]{:S(2)}) collective-permute-start(f32[4,8,2048]{2,1,0:T(8,128)} %get-tuple-element.631), channel_id=1, source_target_pairs={{0,8},{8,16},{16,24},{1,9},{9,17},{17,25},{2,10},{10,18},{18,26},{... | collective-permute-start | bytes 786440 | tf_op jit(solution)/shard_map/while/body/eval_jaxpr/ppermute | solution.py:23
  28.4 6.4 %collective-permute-done.1 = f32[4,8,2048]{2,1,0:T(8,128)S(1)} collective-permute-done((f32[4,8,2048]{2,1,0:T(8,128)}, f32[4,8,2048]{2,1,0:T(8,128)S(1)}, u32[]{:S(2)}, u32[]{:S(2)}) %collective-permute-start.1) | collective-permute-done | bytes 262176 | tf_op jit(solution)/shard_map/while/body/eval_jaxpr/ppermute | solution.py:23
  35.8 1.9 %collective-permute-start.1 = (f32[4,8,2048]{2,1,0:T(8,128)}, f32[4,8,2048]{2,1,0:T(8,128)S(1)}, u32[]{:S(2)}, u32[]{:S(2)}) collective-permute-start(f32[4,8,2048]{2,1,0:T(8,128)} %get-tuple-element.631), channel_id=1, source_target_pairs={{0,8},{8,16},{16,24},{1,9},{9,17},{17,25},{2,10},{10,18},{18,26},{... | collective-permute-start | bytes 786440 | tf_op jit(solution)/shard_map/while/body/eval_jaxpr/ppermute | solution.py:23
  38.4 5.6 %collective-permute-done.1 = f32[4,8,2048]{2,1,0:T(8,128)S(1)} collective-permute-done((f32[4,8,2048]{2,1,0:T(8,128)}, f32[4,8,2048]{2,1,0:T(8,128)S(1)}, u32[]{:S(2)}, u32[]{:S(2)}) %collective-permute-start.1) | collective-permute-done | bytes 262176 | tf_op jit(solution)/shard_map/while/body/eval_jaxpr/ppermute | solution.py:23
  46.6 27.8 %while.32 = (s32[]{:T(128)}, f32[4,8,2048]{2,1,0:T(8,128)S(1)}, f32[4,8,2048]{2,1,0:T(8,128)}, s32[]{:T(128)}, s32[4,1,1]{0,2,1:T(1,128)}, /*index=5*/f32[4,8,2048]{2,1,0:T(8,128)S(1)}, s32[]{:T(128)}, s32[]{:T(128)}) while((s32[]{:T(128)}, f32[4,8,2048]{2,1,0:T(8,128)S(1)}, f32[4,8,2048]{2,1,0:T(8,128)}, s32[]{:T(128)}, ...), condition=%wide.region_1.2_spmd.clone, body=%wide.region_0.0_spmd.clone.sunk | while | flops 327692 | bytes 4188345 | solution.py:99
  46.6 1.9 %collective-permute-start = (f32[4,8,2048]{2,1,0:T(8,128)}, f32[4,8,2048]{2,1,0:T(8,128)S(1)}, u32[]{:S(2)}, u32[]{:S(2)}) collective-permute-start(f32[4,8,2048]{2,1,0:T(8,128)} %get-tuple-element.655), channel_id=1, source_target_pairs={{0,8},{8,16},{16,24},{1,9},{9,17},{17,25},{2,10},{10,18},{18,26},{... | collective-permute-start | bytes 786440 | tf_op jit(solution)/shard_map/while/body/eval_jaxpr/ppermute | solution.py:23
  49.1 5.7 %collective-permute-done = f32[4,8,2048]{2,1,0:T(8,128)S(1)} collective-permute-done((f32[4,8,2048]{2,1,0:T(8,128)}, f32[4,8,2048]{2,1,0:T(8,128)S(1)}, u32[]{:S(2)}, u32[]{:S(2)}) %collective-permute-start) | collective-permute-done | bytes 262176 | tf_op jit(solution)/shard_map/while/body/eval_jaxpr/ppermute | solution.py:23
  55.9 1.9 %collective-permute-start = (f32[4,8,2048]{2,1,0:T(8,128)}, f32[4,8,2048]{2,1,0:T(8,128)S(1)}, u32[]{:S(2)}, u32[]{:S(2)}) collective-permute-start(f32[4,8,2048]{2,1,0:T(8,128)} %get-tuple-element.655), channel_id=1, source_target_pairs={{0,8},{8,16},{16,24},{1,9},{9,17},{17,25},{2,10},{10,18},{18,26},{... | collective-permute-start | bytes 786440 | tf_op jit(solution)/shard_map/while/body/eval_jaxpr/ppermute | solution.py:23
  58.4 5.7 %collective-permute-done = f32[4,8,2048]{2,1,0:T(8,128)S(1)} collective-permute-done((f32[4,8,2048]{2,1,0:T(8,128)}, f32[4,8,2048]{2,1,0:T(8,128)S(1)}, u32[]{:S(2)}, u32[]{:S(2)}) %collective-permute-start) | collective-permute-done | bytes 262176 | tf_op jit(solution)/shard_map/while/body/eval_jaxpr/ppermute | solution.py:23
  65.2 1.9 %collective-permute-start = (f32[4,8,2048]{2,1,0:T(8,128)}, f32[4,8,2048]{2,1,0:T(8,128)S(1)}, u32[]{:S(2)}, u32[]{:S(2)}) collective-permute-start(f32[4,8,2048]{2,1,0:T(8,128)} %get-tuple-element.655), channel_id=1, source_target_pairs={{0,8},{8,16},{16,24},{1,9},{9,17},{17,25},{2,10},{10,18},{18,26},{... | collective-permute-start | bytes 786440 | tf_op jit(solution)/shard_map/while/body/eval_jaxpr/ppermute | solution.py:23
  67.7 5.7 %collective-permute-done = f32[4,8,2048]{2,1,0:T(8,128)S(1)} collective-permute-done((f32[4,8,2048]{2,1,0:T(8,128)}, f32[4,8,2048]{2,1,0:T(8,128)S(1)}, u32[]{:S(2)}, u32[]{:S(2)}) %collective-permute-start) | collective-permute-done | bytes 262176 | tf_op jit(solution)/shard_map/while/body/eval_jaxpr/ppermute | solution.py:23
  75.5 2.2 %fusion.6 = (f32[4,8,2048]{2,1,0:T(8,128)}, f32[4,8,2048]{2,1,0:T(8,128)S(1)}, f32[4,8,2048]{2,1,0:T(8,128)}, f32[4,8,2048]{2,1,0:T(8,128)S(1)}, f32[4,8,2048]{2,1,0:T(8,128)S(1)}, /*index=5*/f32[4,8,2048]{2,1,0:T(8,128)}) fusion(f32[4,8,2047]{2,1,0:T(8,128)S(1)} %mul.319, f32[4,8,2047]{2,1,0:T(8,128)S(1)} %mul.318, f32[8,2048]{1,0:T(8,128)S(1)} %get-tuple-element.529, ...), kind=kLoop, calls=%fused_computation.46 | loop fusion | flops 917504 | bytes 3865872 | tf_op jit(solution)/shard_map/mul | solution.py:105
  83.0 1.1 multiply_multiply_fusion.2
  86.5 1.2 bitcast_convert_fusion
  88.0 1.5 %multiply_multiply_fusion = (f32[4,8,2048]{2,1,0:T(8,128)S(1)}, f32[4,8,2048]{2,1,0:T(8,128)S(1)}) fusion(f32[4,8,2048]{2,1,0:T(8,128)S(1)} %get-tuple-element.310, f32[4,8,2047]{2,1,0:T(8,128)S(1)} %get-tuple-element.394, f32[4,8,2047]{2,1,0:T(8,128)S(1)} %get-tuple-element.393, f32[8,2048]{1,0:T(8,128)S(1)} %get-tuple-element.523, ...), kind=kLoop, calls=%fused_computation.50 | loop fusion | flops 786432 | bytes 3734544 | tf_op jit(solution)/shard_map/mul | solution.py:105
  96.1 1.8 %pad_maximum_fusion = f32[8,4,16384]{2,1,0:T(4,128)} fusion(f32[4,4,16384]{2,1,0:T(4,128)S(1)} %get-tuple-element.482, f32[4,4,16384]{2,1,0:T(4,128)S(1)} %get-tuple-element.481), kind=kLoop, calls=%fused_computation.8 | loop fusion | flops 524288 | bytes 4194304 | tf_op jit(solution)/shard_map/concatenate | solution.py:115
  97.9 3.0 %reshape.147 = f32[8,4,4,4096]{3,2,1,0:T(4,128)S(1)} reshape(f32[8,4,16384]{2,1,0:T(4,128)} %pad_maximum_fusion) | data formatting | bytes 4194304 | tf_op jit(solution)/shard_map/reshape | solution.py:49
  100.9 1.3 slice_select_fusion.1
  102.2 7.1 %collective-permute-start.2 = (f32[8,4,4,2048]{3,2,1,0:T(4,128)}, f32[8,4,4,2048]{3,2,1,0:T(4,128)S(1)}, u32[]{:S(2)}, u32[]{:S(2)}) collective-permute-start(f32[8,4,4,2048]{3,2,1,0:T(4,128)} %slice_select_fusion.1), channel_id=1, source_target_pairs={{0,1},{1,0},{2,3},{3,2},{4,5},{5,4},{6,7},{7,6},{8,9},{9,8},{10,11... | collective-permute-start | bytes 3145736 | tf_op jit(solution)/shard_map/ppermute | solution.py:17
  109.5 2.2 %collective-permute-done.2 = f32[8,4,4,2048]{3,2,1,0:T(4,128)S(1)} collective-permute-done((f32[8,4,4,2048]{3,2,1,0:T(4,128)}, f32[8,4,4,2048]{3,2,1,0:T(4,128)S(1)}, u32[]{:S(2)}, u32[]{:S(2)}) %collective-permute-start.2) | collective-permute-done | bytes 1048608 | tf_op jit(solution)/shard_map/ppermute | solution.py:17
  112.4 1.7 %multiply_add_fusion = f32[8,4,4,2048]{3,2,1,0:T(4,128)} fusion(f32[8,4,4,2048]{3,2,1,0:T(4,128)S(1)} %collective-permute-done.2, f32[8,4,2048]{2,1,0:T(4,128)S(1)} %fusion.7, pred[4,2048]{1,0:T(4,128)(4,1)S(1)} %get-tuple-element.307, f32[8,4,4,4096]{3,2,1,0:T(4,128)S(1)} %reshape.147, pred[]{:T(512)S(6)} %eq.188), kind=kLoop, calls=%fused_computation.9 | loop fusion | flops 1310720 | bytes 4464641 | tf_op jit(solution)/shard_map/add | solution.py:61
  114.1 2.3 %reshape_reshape.15 = f32[8,4,2,4096]{3,2,1,0:T(2,128)S(1)} reshape(f32[8,4,4,2048]{3,2,1,0:T(4,128)} %multiply_add_fusion) | data formatting | bytes 2097152 | tf_op jit(solution)/shard_map/reshape;reshape | solution.py:49
  116.7 1.4 collective-permute-start.3
  118.1 11.8 %collective-permute-done.3 = f32[8,4,2,2048]{3,2,1,0:T(2,128)S(1)} collective-permute-done((f32[8,4,2,2048]{3,2,1,0:T(2,128)S(1)}, f32[8,4,2,2048]{3,2,1,0:T(2,128)S(1)}, u32[]{:S(2)}, u32[]{:S(2)}) %collective-permute-start.3) | collective-permute-done | bytes 524320 | tf_op jit(solution)/shard_map/ppermute | solution.py:17
  131.8 2.4 %collective-permute-start.4 = (f32[8,4,1,2048]{3,1,0,2:T(4,128)S(1)}, f32[8,4,1,2048]{3,1,0,2:T(4,128)S(1)}, u32[]{:S(2)}, u32[]{:S(2)}) collective-permute-start(f32[8,4,1,2048]{3,1,0,2:T(4,128)S(1)} %slice_select_fusion.3), channel_id=1, source_target_pairs={{0,4},{1,5},{2,6},{3,7},{4,0},{5,1},{6,2},{7,3},{8,12},{9,13},{10,... | collective-permute-start | bytes 786440 | tf_op jit(solution)/shard_map/ppermute | solution.py:17
  134.3 11.3 %collective-permute-done.4 = f32[8,4,1,2048]{3,1,0,2:T(4,128)S(1)} collective-permute-done((f32[8,4,1,2048]{3,1,0,2:T(4,128)S(1)}, f32[8,4,1,2048]{3,1,0,2:T(4,128)S(1)}, u32[]{:S(2)}, u32[]{:S(2)}) %collective-permute-start.4) | collective-permute-done | bytes 262176 | tf_op jit(solution)/shard_map/ppermute | solution.py:17
  (233 shorter events, 41.0 us)
Async XLA Ops:
  0.0 2.6 %copy-start.46 = (s32[8]{0:T(128)S(1)}, s32[8]{0:T(128)}, u32[]{:S(2)}) copy-start(s32[8]{0:T(128)} %param.12) | copy-start | bytes 100
  14.3 10.2 %collective-permute-start.1 = (f32[4,8,2048]{2,1,0:T(8,128)}, f32[4,8,2048]{2,1,0:T(8,128)S(1)}, u32[]{:S(2)}, u32[]{:S(2)}) collective-permute-start(f32[4,8,2048]{2,1,0:T(8,128)} %get-tuple-element.631), channel_id=1, source_target_pairs={{0,8},{8,16},{16,24},{1,9},{9,17},{17,25},{2,10},{10,18},{18,26},{... | collective-permute-start | bytes 786440 | tf_op jit(solution)/shard_map/while/body/eval_jaxpr/ppermute | solution.py:23
  25.5 9.2 %collective-permute-start.1 = (f32[4,8,2048]{2,1,0:T(8,128)}, f32[4,8,2048]{2,1,0:T(8,128)S(1)}, u32[]{:S(2)}, u32[]{:S(2)}) collective-permute-start(f32[4,8,2048]{2,1,0:T(8,128)} %get-tuple-element.631), channel_id=1, source_target_pairs={{0,8},{8,16},{16,24},{1,9},{9,17},{17,25},{2,10},{10,18},{18,26},{... | collective-permute-start | bytes 786440 | tf_op jit(solution)/shard_map/while/body/eval_jaxpr/ppermute | solution.py:23
  35.8 8.2 %collective-permute-start.1 = (f32[4,8,2048]{2,1,0:T(8,128)}, f32[4,8,2048]{2,1,0:T(8,128)S(1)}, u32[]{:S(2)}, u32[]{:S(2)}) collective-permute-start(f32[4,8,2048]{2,1,0:T(8,128)} %get-tuple-element.631), channel_id=1, source_target_pairs={{0,8},{8,16},{16,24},{1,9},{9,17},{17,25},{2,10},{10,18},{18,26},{... | collective-permute-start | bytes 786440 | tf_op jit(solution)/shard_map/while/body/eval_jaxpr/ppermute | solution.py:23
  46.6 8.2 %collective-permute-start = (f32[4,8,2048]{2,1,0:T(8,128)}, f32[4,8,2048]{2,1,0:T(8,128)S(1)}, u32[]{:S(2)}, u32[]{:S(2)}) collective-permute-start(f32[4,8,2048]{2,1,0:T(8,128)} %get-tuple-element.655), channel_id=1, source_target_pairs={{0,8},{8,16},{16,24},{1,9},{9,17},{17,25},{2,10},{10,18},{18,26},{... | collective-permute-start | bytes 786440 | tf_op jit(solution)/shard_map/while/body/eval_jaxpr/ppermute | solution.py:23
  55.9 8.2 %collective-permute-start = (f32[4,8,2048]{2,1,0:T(8,128)}, f32[4,8,2048]{2,1,0:T(8,128)S(1)}, u32[]{:S(2)}, u32[]{:S(2)}) collective-permute-start(f32[4,8,2048]{2,1,0:T(8,128)} %get-tuple-element.655), channel_id=1, source_target_pairs={{0,8},{8,16},{16,24},{1,9},{9,17},{17,25},{2,10},{10,18},{18,26},{... | collective-permute-start | bytes 786440 | tf_op jit(solution)/shard_map/while/body/eval_jaxpr/ppermute | solution.py:23
  65.2 8.2 %collective-permute-start = (f32[4,8,2048]{2,1,0:T(8,128)}, f32[4,8,2048]{2,1,0:T(8,128)S(1)}, u32[]{:S(2)}, u32[]{:S(2)}) collective-permute-start(f32[4,8,2048]{2,1,0:T(8,128)} %get-tuple-element.655), channel_id=1, source_target_pairs={{0,8},{8,16},{16,24},{1,9},{9,17},{17,25},{2,10},{10,18},{18,26},{... | collective-permute-start | bytes 786440 | tf_op jit(solution)/shard_map/while/body/eval_jaxpr/ppermute | solution.py:23
  75.5 2.5 %copy-start.36 = (f32[1,8,2048]{2,0,1:T(1,128)S(1)}, f32[1,8,2048]{2,0,1:T(1,128)}, u32[]{:S(2)}) copy-start(f32[1,8,2048]{2,0,1:T(1,128)} %get-tuple-element.379) | copy-start | bytes 196612
  75.5 2.5 %copy-start.37 = (f32[1,8,2048]{2,0,1:T(1,128)S(1)}, f32[1,8,2048]{2,0,1:T(1,128)}, u32[]{:S(2)}) copy-start(f32[1,8,2048]{2,0,1:T(1,128)} %get-tuple-element.380) | copy-start | bytes 196612
  84.4 2.1 %copy-start.24 = (bf16[3,8,8,2048]{3,2,1,0:T(8,128)(2,1)S(1)}, bf16[3,8,8,2048]{3,2,1,0:T(8,128)(2,1)}, u32[]{:S(2)}) copy-start(bf16[3,8,8,2048]{3,2,1,0:T(8,128)(2,1)} %param.10) | copy-start | bytes 2359300
  85.5 2.2 %copy-start.47 = (f32[8,3]{0,1:T(4,128)S(1)}, f32[8,3]{0,1:T(4,128)}, u32[]{:S(2)}) copy-start(f32[8,3]{0,1:T(4,128)} %param.11) | copy-start | bytes 292
  88.0 2.2 %copy-start.2 = (f32[4,8,2048]{2,1,0:T(8,128)S(1)}, f32[4,8,2048]{2,1,0:T(8,128)}, u32[]{:S(2)}) copy-start(f32[4,8,2048]{2,1,0:T(8,128)} %get-tuple-element.329) | copy-start | bytes 786436
  88.0 2.2 %copy-start.3 = (f32[4,8,2048]{2,1,0:T(8,128)S(1)}, f32[4,8,2048]{2,1,0:T(8,128)}, u32[]{:S(2)}) copy-start(f32[4,8,2048]{2,1,0:T(8,128)} %get-tuple-element.371) | copy-start | bytes 786436
  88.0 2.2 %copy-start.31 = (f32[3,8,2048]{2,1,0:T(8,128)S(1)}, f32[3,8,2048]{2,1,0:T(8,128)}, u32[]{:S(2)}) copy-start(f32[3,8,2048]{2,1,0:T(8,128)} %get-tuple-element.366) | copy-start | bytes 589828
  88.0 2.8 %copy-start.14 = (f32[4,8,2048]{2,1,0:T(8,128)S(1)}, f32[4,8,2048]{2,1,0:T(8,128)}, u32[]{:S(2)}) copy-start(f32[4,8,2048]{2,1,0:T(8,128)} %get-tuple-element.325) | copy-start | bytes 786436
  88.0 2.8 %copy-start.15 = (f32[4,8,2048]{2,1,0:T(8,128)S(1)}, f32[4,8,2048]{2,1,0:T(8,128)}, u32[]{:S(2)}) copy-start(f32[4,8,2048]{2,1,0:T(8,128)} %get-tuple-element.467) | copy-start | bytes 786436
  88.0 2.8 %copy-start.30 = (f32[3,8,2048]{2,1,0:T(8,128)S(1)}, f32[3,8,2048]{2,1,0:T(8,128)}, u32[]{:S(2)}) copy-start(f32[3,8,2048]{2,1,0:T(8,128)} %get-tuple-element.365) | copy-start | bytes 589828
  89.6 2.3 %copy-start.18 = (f32[4,8,2048]{2,1,0:T(8,128)S(1)}, f32[4,8,2048]{2,1,0:T(8,128)}, u32[]{:S(2)}) copy-start(f32[4,8,2048]{2,1,0:T(8,128)} %get-tuple-element.317) | copy-start | bytes 786436
  89.6 2.3 %copy-start.19 = (f32[4,8,2048]{2,1,0:T(8,128)S(1)}, f32[4,8,2048]{2,1,0:T(8,128)}, u32[]{:S(2)}) copy-start(f32[4,8,2048]{2,1,0:T(8,128)} %get-tuple-element.463) | copy-start | bytes 786436
  89.6 2.3 %copy-start.28 = (f32[3,8,2048]{2,1,0:T(8,128)S(1)}, f32[3,8,2048]{2,1,0:T(8,128)}, u32[]{:S(2)}) copy-start(f32[3,8,2048]{2,1,0:T(8,128)} %get-tuple-element.363) | copy-start | bytes 589828
  90.1 2.3 %copy-start.20 = (f32[4,8,2048]{2,1,0:T(8,128)S(1)}, f32[4,8,2048]{2,1,0:T(8,128)}, u32[]{:S(2)}) copy-start(f32[4,8,2048]{2,1,0:T(8,128)} %get-tuple-element.313) | copy-start | bytes 786436
  90.2 2.3 %copy-start.21 = (f32[4,8,2048]{2,1,0:T(8,128)S(1)}, f32[4,8,2048]{2,1,0:T(8,128)}, u32[]{:S(2)}) copy-start(f32[4,8,2048]{2,1,0:T(8,128)} %get-tuple-element.461) | copy-start | bytes 786436
  90.2 2.3 %copy-start.27 = (f32[3,8,2048]{2,1,0:T(8,128)S(1)}, f32[3,8,2048]{2,1,0:T(8,128)}, u32[]{:S(2)}) copy-start(f32[3,8,2048]{2,1,0:T(8,128)} %get-tuple-element.362) | copy-start | bytes 589828
  90.7 2.3 %copy-start.22 = (f32[4,8,2048]{2,1,0:T(8,128)S(1)}, f32[4,8,2048]{2,1,0:T(8,128)}, u32[]{:S(2)}) copy-start(f32[4,8,2048]{2,1,0:T(8,128)} %get-tuple-element.309) | copy-start | bytes 786436
  90.7 2.3 %copy-start.23 = (f32[4,8,2048]{2,1,0:T(8,128)S(1)}, f32[4,8,2048]{2,1,0:T(8,128)}, u32[]{:S(2)}) copy-start(f32[4,8,2048]{2,1,0:T(8,128)} %get-tuple-element.459) | copy-start | bytes 786436
  90.8 2.3 %copy-start.26 = (f32[3,8,2048]{2,1,0:T(8,128)S(1)}, f32[3,8,2048]{2,1,0:T(8,128)}, u32[]{:S(2)}) copy-start(f32[3,8,2048]{2,1,0:T(8,128)} %get-tuple-element.368) | copy-start | bytes 589828
  91.3 2.3 %copy-start.1 = (f32[4,8,2048]{2,1,0:T(8,128)S(1)}, f32[4,8,2048]{2,1,0:T(8,128)}, u32[]{:S(2)}) copy-start(f32[4,8,2048]{2,1,0:T(8,128)} %get-tuple-element.392) | copy-start | bytes 786436
  91.3 2.3 %copy-start.25 = (f32[3,8,2048]{2,1,0:T(8,128)S(1)}, f32[3,8,2048]{2,1,0:T(8,128)}, u32[]{:S(2)}) copy-start(f32[3,8,2048]{2,1,0:T(8,128)} %get-tuple-element.367) | copy-start | bytes 589828
  100.9 8.4 %copy-start.49 = (s32[8]{0:T(128)S(1)}, s32[8]{0:T(128)}, u32[]{:S(2)}) copy-start(s32[8]{0:T(128)} %param.13) | copy-start | bytes 100
  102.2 9.6 %collective-permute-start.2 = (f32[8,4,4,2048]{3,2,1,0:T(4,128)}, f32[8,4,4,2048]{3,2,1,0:T(4,128)S(1)}, u32[]{:S(2)}, u32[]{:S(2)}) collective-permute-start(f32[8,4,4,2048]{3,2,1,0:T(4,128)} %slice_select_fusion.1), channel_id=1, source_target_pairs={{0,1},{1,0},{2,3},{3,2},{4,5},{5,4},{6,7},{7,6},{8,9},{9,8},{10,11... | collective-permute-start | bytes 3145736 | tf_op jit(solution)/shard_map/ppermute | solution.py:17
  116.7 13.2 %collective-permute-start.3 = (f32[8,4,2,2048]{3,2,1,0:T(2,128)S(1)}, f32[8,4,2,2048]{3,2,1,0:T(2,128)S(1)}, u32[]{:S(2)}, u32[]{:S(2)}) collective-permute-start(f32[8,4,2,2048]{3,2,1,0:T(2,128)S(1)} %broadcast_select_fusion.2), channel_id=1, source_target_pairs={{0,2},{1,3},{2,0},{3,1},{4,6},{5,7},{6,4},{7,5},{8,10},{9,11},{10,... | collective-permute-start | bytes 1572872 | tf_op jit(solution)/shard_map/ppermute | solution.py:17
  131.8 13.7 %collective-permute-start.4 = (f32[8,4,1,2048]{3,1,0,2:T(4,128)S(1)}, f32[8,4,1,2048]{3,1,0,2:T(4,128)S(1)}, u32[]{:S(2)}, u32[]{:S(2)}) collective-permute-start(f32[8,4,1,2048]{3,1,0,2:T(4,128)S(1)} %slice_select_fusion.3), channel_id=1, source_target_pairs={{0,4},{1,5},{2,6},{3,7},{4,0},{5,1},{6,2},{7,3},{8,12},{9,13},{10,... | collective-permute-start | bytes 786440 | tf_op jit(solution)/shard_map/ppermute | solution.py:17
  (27 other events, 34.2 us)
where the time goes:
time: 148 us; the launch traced here: 147 us
  waiting for transfers between devices  60.8 us (41%)
  other arithmetic  42.3 us (29%)
  starting transfers between devices  23.7 us (16%)
  local copies, waits for them, and re-layouts  18.3 us (12%)
    ppermute x6, waiting for transfers between devices, shifted(): lax.ppermute(value, axis, [(source, source + steps) for source in range(l...  35.5 us
    ppermute x3, waiting for transfers between devices, partner(): return lax.ppermute(value, axis, pairs)  25.3 us
    ppermute x6, starting transfers between devices, shifted(): lax.ppermute(value, axis, [(source, source + steps) for source in range(l...  12.9 us
    ppermute x3, starting transfers between devices, partner(): return lax.ppermute(value, axis, pairs)  10.8 us
    mul x7, other arithmetic, local(): current * partial_value[slice_index] * weights[slice_index][None]  9.03 us
    slice x35, local copies, waits for them, and re-layouts, move_cells(): return jnp.concatenate([filler, planes[..., :columns - amount]], axis=-1)  6 us
    mul x7, other arithmetic, local(): exit_part * extinction[slice_index][None]  5.65 us
    mul x6, other arithmetic, hop_once(): slide_cells(entering_now, lateral, slices) * exit_part  5.07 us
  transfers between devices with their start and end apart: 9, of which 9 were waited for; matrix products, arithmetic and copies ran while one was open for 3% of the time, Pallas kernels for 0%

commit v1 on v0

v1 whole, which is shorter than its diff:
```python
import functools
import jax
import jax.numpy as jnp
from jax import lax
from jax.experimental import pallas as pl
from jax.experimental.pallas import tpu as pltpu
from jax.sharding import PartitionSpec as P

LIGHT_DEPTH = 1.5
VIEW_DEPTH = 2.0
LANES = 128
SUB = 8
SHIFTS = (-1, 0, 1)
MESH = pl.DeviceIdType.MESH


def chunked(plane):
    return jnp.stack([plane[:, k : k + LANES] for k in range(0, plane.shape[1], LANES)])


def slide(planes, amount, fill):
    if amount == 0:
        return planes
    count = planes.shape[0]
    whole, part = divmod(abs(amount), LANES)
    whole = min(whole, count)
    lane = lax.broadcasted_iota(jnp.int32, planes.shape, 2)

    def blocks(n):
        return [jnp.full((n,) + planes.shape[1:], fill, planes.dtype)] if n else []

    if amount > 0:
        if whole:
            planes = jnp.concatenate(blocks(whole) + [planes[: count - whole]] * (whole < count), axis=0)
        if part:
            turned = pltpu.roll(planes, part, 2)
            before = jnp.concatenate(blocks(1) + [turned[:-1]], axis=0)
            planes = jnp.where(lane < part, before, turned)
    else:
        if whole:
            planes = jnp.concatenate([planes[whole:]] * (whole < count) + blocks(whole), axis=0)
        if part:
            turned = pltpu.roll(planes, LANES - part, 2)
            after = jnp.concatenate([turned[1:]] + blocks(1), axis=0)
            planes = jnp.where(lane >= LANES - part, after, turned)
    return planes


def column_sums(planes):
    for bit in (1, 2, 4):
        pairs = planes.reshape(planes.shape[0] // 2, 2, SUB, LANES)
        even, odd = pairs[:, 0], pairs[:, 1]
        row = lax.broadcasted_iota(jnp.int32, even.shape, 1)
        first = (row & bit) == 0
        planes = jnp.where(first, even, odd) + pltpu.roll(jnp.where(first, odd, even), SUB - bit, 1)
    return planes.reshape(planes.shape[0] * SUB, LANES)


def kernel(
    light_count, view_count, density_ref, albedo_ref, flip_ref, out_ref,
    ext, lit, exits, slots, part, part_total, swap, swap_total, comb, comb_total, got, got_total, rows4,
    exit_send, exit_recv, core_send, core_recv, z_send, z_recv,
):
    slices, cells, columns = density_ref.shape
    z_count = view_count // 2
    chunks = columns // LANES
    rows = got.shape[3]
    per_slice = chunks // rows
    light_step = LIGHT_DEPTH / (slices * light_count)
    view_step = VIEW_DEPTH / (cells * view_count)
    me_light = lax.axis_index("light")
    me_view = lax.axis_index("view")
    core = lax.rem(me_view, 2)
    z = lax.div(me_view, 2)
    other = 1 - core

    barrier = pltpu.get_barrier_semaphore()
    for step in range(1, light_count):
        pl.semaphore_signal(barrier, inc=1, device_id=(lax.rem(me_light + step, light_count), me_view), device_id_type=MESH)
    pl.semaphore_signal(barrier, inc=1, device_id=(me_light, z * 2 + other), device_id_type=MESH)
    for step in range(1, z_count):
        pl.semaphore_signal(barrier, inc=1, device_id=(me_light, lax.rem(z + step, z_count) * 2 + core), device_id_type=MESH)

    def fade(x, carry):
        ext[x] = jnp.exp(-chunked(density_ref[x]) * light_step)
        return carry

    lax.fori_loop(0, slices, fade, 0)
    for a, amount in enumerate(SHIFTS):
        exits[a] = lax.fori_loop(
            0, slices, lambda x, e: slide(e * ext[x], amount, 1.0), jnp.ones(ext.shape[1:], jnp.float32)
        )
    for hop in range(light_count - 1):

        @pl.when(hop >= me_light)
        def _():
            for a in range(3):
                slots[a, hop] = jnp.ones(slots.shape[2:], jnp.float32)

    pl.semaphore_wait(barrier, light_count - 1 + 1 + z_count - 1)

    def exit_copy(a, hop):
        return pltpu.make_async_remote_copy(
            src_ref=exits.at[a], dst_ref=slots.at[a, hop],
            send_sem=exit_send.at[a, hop], recv_sem=exit_recv.at[a, hop],
            device_id=(lax.rem(me_light + hop + 1, light_count), me_view), device_id_type=MESH,
        )

    for a in range(3):
        for hop in range(light_count - 1):

            @pl.when(me_light + hop + 1 < light_count)
            def _():
                exit_copy(a, hop).start()

    cell = lax.broadcasted_iota(jnp.int32, (chunks, cells, LANES), 1)

    def weigh(x, carry):
        depth = chunked(density_ref[x]) * view_step
        running = depth
        for step in (1, 2, 4):
            running = running + jnp.where(cell >= step, pltpu.roll(running, step, 1), 0.0)
        suffix = depth
        for step in (1, 2, 4):
            suffix = suffix + jnp.where(cell < cells - step, pltpu.roll(suffix, cells - step, 1), 0.0)
        ahead = jnp.where(flip_ref[x] == 1, suffix, running) - depth
        weight = jnp.exp(-ahead) * (1.0 - jnp.exp(-depth))
        for c in range(3):
            lit[c, x] = weight * chunked(albedo_ref[c, x].astype(jnp.float32))
        total = column_sums(depth)
        for j in range(per_slice):
            piece = x * per_slice + j
            part_total[lax.rem(piece, 2), lax.div(piece, 2)] = total[j * rows : (j + 1) * rows]
        return carry

    lax.fori_loop(0, slices, weigh, 0)

    def core_copy(src, dst, index):
        return pltpu.make_async_remote_copy(
            src_ref=src, dst_ref=dst, send_sem=core_send.at[index], recv_sem=core_recv.at[index],
            device_id=(me_light, z * 2 + other), device_id_type=MESH,
        )

    total_swap = core_copy(part_total.at[other], swap_total, 3)
    total_swap.start()

    def z_copy(src, dst, index, step):
        return pltpu.make_async_remote_copy(
            src_ref=src, dst_ref=dst, send_sem=z_send.at[index, step], recv_sem=z_recv.at[index, z],
            device_id=(me_light, lax.rem(z + step, z_count) * 2 + core), device_id_type=MESH,
        )

    def z_wait(dst, index, step):
        source = lax.rem(z + step, z_count)
        pltpu.make_async_remote_copy(
            src_ref=dst.at[source], dst_ref=dst.at[source], send_sem=z_send.at[index, step],
            recv_sem=z_recv.at[index, source], device_id=(me_light, source * 2 + core), device_id_type=MESH,
        ).wait_recv()

    def flip_of(piece):
        return flip_ref[lax.div(piece, per_slice)]

    total_swap.wait_recv()
    comb_total[...] = part_total[core] + swap_total[...]
    sends = []
    for step in range(1, z_count):
        copy = z_copy(comb_total.at[lax.rem(z + step, z_count)], got_total.at[z], 3, step)
        copy.start()
        sends.append(copy)
    got_total[z] = comb_total[z]

    def enter(a, amount):
        for hop in range(light_count - 1):

            @pl.when(hop < me_light)
            def _():
                exit_copy(a, hop).wait_recv()

        entering = slots[a, light_count - 2]
        for hop in range(light_count - 3, -1, -1):
            entering = slide(entering, amount * slices, 1.0) * slots[a, hop]
        return entering

    def march(a, amount):
        def one(x, trans):
            for c in range(3):
                sums = column_sums(trans * lit[c, x])
                for j in range(per_slice):
                    piece = x * per_slice + j
                    part[a, lax.rem(piece, 2), lax.div(piece, 2), c] = sums[j * rows : (j + 1) * rows]
            return slide(trans * ext[x], amount, 1.0)

        lax.fori_loop(0, slices, one, enter(a, amount))

    def join(a):
        def one(target, carry):
            flip = flip_of(target * 2 + core)
            mine_first = flip == core
            mine_fade = jnp.where(mine_first, 1.0, jnp.exp(-swap_total[target]))
            their_fade = jnp.where(mine_first, jnp.exp(-part_total[core, target]), 1.0)
            for c in range(3):
                comb[a, target, c] = mine_fade * part[a, core, target, c] + their_fade * swap[a, target, c]
            return carry

        lax.fori_loop(0, z_count, one, 0)

    swaps = []

    def finish_swap(a):
        swaps[a].wait_recv()
        join(a)
        for step in range(1, z_count):
            copy = z_copy(comb.at[a, lax.rem(z + step, z_count)], got.at[a, z], a, step)
            copy.start()
            sends.append(copy)
        got[a, z] = comb[a, z]

    for a, amount in enumerate(SHIFTS):
        march(a, amount)
        copy = core_copy(part.at[a, other], swap.at[a], a)
        copy.start()
        swaps.append(copy)
        if a > 0:
            finish_swap(a - 1)
    finish_swap(2)

    for step in range(1, z_count):
        z_wait(got_total, 3, step)
    flip = flip_of(me_view)
    before = jnp.zeros(got_total.shape[1:], jnp.float32)
    fades = []
    for source in range(z_count):
        fades.append(before)
        before = before + got_total[source]
    for source in range(z_count):
        depth = jnp.where(flip == 1, before - fades[source] - got_total[source], fades[source])
        fades[source] = jnp.exp(-depth)
    opacity = 1.0 - jnp.exp(-before)
    for a in range(3):
        for step in range(1, z_count):
            z_wait(got.at[a], a, step)
        for c in range(3):
            value = fades[0] * got[a, 0, c]
            for source in range(1, z_count):
                value = value + fades[source] * got[a, source, c]
            rows4[a, pl.ds(c, rows, stride=4), :] = value
        rows4[a, pl.ds(3, rows, stride=4), :] = opacity
        for r in range(rows):
            out_ref[a, :, r * LANES : (r + 1) * LANES] = rows4[a, r * 4 : (r + 1) * 4, :]

    for copy in sends:
        copy.wait_send()
    for copy in swaps:
        copy.wait_send()
    total_swap.wait_send()
    for a in range(3):
        for hop in range(light_count - 1):

            @pl.when(me_light + hop + 1 < light_count)
            def _():
                exit_copy(a, hop).wait_send()


def local(density, albedo, light_color, light_shift, view_flip):
    slices, cells, columns = density.shape
    light_count = lax.axis_size("light")
    view_count = lax.axis_size("view")
    z_count = view_count // 2
    chunks = columns // LANES
    piece = slices * columns // view_count
    rows = piece // LANES
    f32 = jnp.float32
    vmem = pl.BlockSpec(memory_space=pltpu.VMEM)
    dma = pltpu.SemaphoreType.DMA
    planes = pl.pallas_call(
        functools.partial(kernel, light_count, view_count),
        out_shape=jax.ShapeDtypeStruct((3, 4, piece), f32),
        in_specs=[vmem, vmem, pl.BlockSpec(memory_space=pltpu.SMEM)],
        out_specs=vmem,
        scratch_shapes=[
            pltpu.VMEM((slices, chunks, cells, LANES), f32),
            pltpu.VMEM((3, slices, chunks, cells, LANES), f32),
            pltpu.VMEM((3, chunks, cells, LANES), f32),
            pltpu.VMEM((3, light_count - 1, chunks, cells, LANES), f32),
            pltpu.VMEM((3, 2, z_count, 3, rows, LANES), f32),
            pltpu.VMEM((2, z_count, rows, LANES), f32),
            pltpu.VMEM((3, z_count, 3, rows, LANES), f32),
            pltpu.VMEM((z_count, rows, LANES), f32),
            pltpu.VMEM((3, z_count, 3, rows, LANES), f32),
            pltpu.VMEM((z_count, rows, LANES), f32),
            pltpu.VMEM((3, z_count, 3, rows, LANES), f32),
            pltpu.VMEM((z_count, rows, LANES), f32),
            pltpu.VMEM((3, rows * 4, LANES), f32),
            dma((3, light_count - 1)),
            dma((3, light_count - 1)),
            dma((4,)),
            dma((4,)),
            dma((4, z_count)),
            dma((4, z_count)),
        ],
        compiler_params=pltpu.CompilerParams(
            collective_id=0, has_side_effects=True, vmem_limit_bytes=32 * 2**20
        ),
    )(density, albedo, view_flip)
    lateral = light_shift[:, None, None]
    picked = jnp.where(lateral == 1, planes[2][None], jnp.where(lateral == -1, planes[0][None], planes[1][None]))
    tint = jnp.concatenate([light_color, jnp.ones((light_color.shape[0], 1), f32)], axis=1)
    return picked * tint[:, :, None]


def solution(mesh):
    return jax.shard_map(
        local,
        mesh=mesh,
        in_specs=(P("light", "view", None), P(None, "light", "view", None), P(), P(), P("light")),
        out_specs=P(None, None, ("light", "view")),
        check_vma=False,
    )
```

time: 148 us -> 27.7 us (0.19)
  waiting for transfers between devices: 60.8 us -> 0 us
  other arithmetic: 42.3 us -> 1.57 us
  starting transfers between devices: 23.7 us -> 0 us
  Pallas kernels: 0 us -> 22.2 us
  local copies, waits for them, and re-layouts: 18.3 us -> 3.6 us
    ppermute x9 -> x0, waiting for transfers between devices: 60.8 us -> none  [the longest x6 35.5 us: shifted(): lax.ppermute(value, axis, [(source, source + steps) for source in range(l...]
    ppermute x9 -> x0, starting transfers between devices: 23.7 us -> none  [the longest x6 12.9 us: shifted(): lax.ppermute(value, axis, [(source, source + steps) for source in range(l...]
    pallas_call x0 -> x1, Pallas kernels: none -> 22.2 us  [local(): pl.pallas_call(functools.partial(kernel, light_count, view_count), out_sh...]
    mul x25 -> x1, other arithmetic: 21 us -> 0.91 us  [local(): return picked * tint[:, :, None]]
    slice x40 -> x0, local copies, waits for them, and re-layouts: 7.99 us -> none  [the longest x35 6 us: move_cells(): return jnp.concatenate([filler, planes[..., :columns - amount]], axis=-1)]
    reduce_sum x8 -> x0, other arithmetic: 4.25 us -> none  [local(): colour = jnp.sum(reflect[None] * lit_cells[:, None], axis=2)]
    select_n x13 -> x0, other arithmetic: 3.52 us -> none  [the longest x3 1.65 us: binary_swap(): outgoing = jnp.where(own_bit == 1, lower_half, upper_half)]
    eq x8 -> x1, other arithmetic: 3.8 us -> 0.66 us  [local(): lateral == 1]
  transfers between devices with their start and end apart: 9 -> 0, of which waited for: 9 -> 0; matrix products, arithmetic and copies ran while one was open for 3% -> 0% of each run, Pallas kernels for 0% -> 0%
where the time goes in v1:
time: 27.7 us; the launch traced here: 27.4 us
  Pallas kernels  22.2 us (80%)
  local copies, waits for them, and re-layouts  3.6 us (13%)
  other arithmetic  1.57 us (6%)
    pallas_call x1, Pallas kernels, local(): pl.pallas_call(functools.partial(kernel, light_count, view_count), out_sh...  22.2 us
    unnamed x9, local copies, waits for them, and re-layouts  3.58 us
    mul x1, other arithmetic, local(): return picked * tint[:, :, None]  0.91 us
    eq x1, other arithmetic, local(): lateral == 1  0.66 us

profile of v1, /device:TPU:5, one launch (start us, length us, event | category | flops | bytes accessed | tf_op | source)
XLA Modules:
  0.0 27.4 jit_solution(7897560784224880877)
XLA Ops:
  0.0 0.7 %broadcast_compare_fusion.1 = (pred[8]{0:T(512)(128)(4,1)S(1)}, pred[8]{0:T(512)(128)(4,1)S(1)}) fusion(s32[8]{0:T(128)} %param.8), kind=kLoop, calls=%fused_computation.5 | loop fusion | flops 16 | bytes 48 | tf_op jit(solution)/shard_map/eq | solution.py:306
  0.7 0.0 copy-start.3
  0.7 0.7 %copy-done.3 = f32[8,3]{0,1:T(4,128)S(1)} copy-done((f32[8,3]{0,1:T(4,128)S(1)}, f32[8,3]{0,1:T(4,128)}, u32[]{:S(2)}) %copy-start.3) | copy-done | bytes 120
  1.3 0.1 copy.7
  1.4 0.0 copy-start.2
  1.4 0.6 %copy-done.2 = s32[8]{0:T(128)S(1)} copy-done((s32[8]{0:T(128)S(1)}, s32[8]{0:T(128)}, u32[]{:S(2)}) %copy-start.2) | copy-done | bytes 56
  2.1 0.0 copy-start
  2.1 1.1 %copy-done = bf16[3,8,8,2048]{3,2,1,0:T(8,128)(2,1)S(1)} copy-done((bf16[3,8,8,2048]{3,2,1,0:T(8,128)(2,1)S(1)}, bf16[3,8,8,2048]{3,2,1,0:T(8,128)(2,1)}, u32[]{:S(2)}) %copy-start) | copy-done | bytes 786456
  3.2 0.0 copy-start.1
  3.2 1.0 %copy-done.1 = f32[8,8,2048]{2,1,0:T(8,128)S(1)} copy-done((f32[8,8,2048]{2,1,0:T(8,128)S(1)}, f32[8,8,2048]{2,1,0:T(8,128)}, u32[]{:S(2)}) %copy-start.1) | copy-done | bytes 524312
  4.3 22.2 %shard_map.55 = f32[3,4,2048]{2,1,0:T(4,128)S(1)} custom-call(f32[8,8,2048]{2,1,0:T(8,128)S(1)} %copy-done.1, bf16[3,8,8,2048]{3,2,1,0:T(8,128)(2,1)S(1)} %copy-done, s32[8]{0:T(128)S(1)} %copy-done.2), custom_call_target="tpu_custom_call" | custom-call | tf_op jit(solution)/shard_map/pallas_call | solution.py:275
  26.5 0.9 %select_multiply_fusion = f32[8,4,2048]{2,1,0:T(4,128)} fusion(f32[8,4]{1,0:T(8,128)S(1)} %concatenate.3.clone, f32[4,2048]{1,0:T(4,128)S(1)} %get-tuple-element.6, f32[4,2048]{1,0:T(4,128)S(1)} %get-tuple-element.7, f32[4,2048]{1,0:T(4,128)S(1)} %get-tuple-element.5, pred[8]{0:T(512)(128)(4,1)S(1)} %get-tuple-element.9, pred[8]{0:T(512)(128)(4,1)S(1)} %get-tuple-element.8), kind=kLoop, calls=%fused_computation | loop fusion | flops 196608 | bytes 360592 | tf_op jit(solution)/shard_map/mul | solution.py:308
  (2 shorter events, 0.0 us)
Async XLA Ops:
  0.7 0.7 %copy-start.3 = (f32[8,3]{0,1:T(4,128)S(1)}, f32[8,3]{0,1:T(4,128)}, u32[]{:S(2)}) copy-start(f32[8,3]{0,1:T(4,128)} %param.7) | copy-start | bytes 292
  1.4 0.7 %copy-start.2 = (s32[8]{0:T(128)S(1)}, s32[8]{0:T(128)}, u32[]{:S(2)}) copy-start(s32[8]{0:T(128)} %flip_ref.1) | copy-start | bytes 100
  2.1 1.1 %copy-start = (bf16[3,8,8,2048]{3,2,1,0:T(8,128)(2,1)S(1)}, bf16[3,8,8,2048]{3,2,1,0:T(8,128)(2,1)}, u32[]{:S(2)}) copy-start(bf16[3,8,8,2048]{3,2,1,0:T(8,128)(2,1)} %albedo_ref.1) | copy-start | bytes 2359300
  3.2 1.0 %copy-start.1 = (f32[8,8,2048]{2,1,0:T(8,128)S(1)}, f32[8,8,2048]{2,1,0:T(8,128)}, u32[]{:S(2)}) copy-start(f32[8,8,2048]{2,1,0:T(8,128)} %density_ref.1) | copy-start | bytes 1572868

commit v2 on v1

v2 whole, which is shorter than its diff:
```python
import functools
import jax
import jax.numpy as jnp
from jax import lax
from jax.experimental import pallas as pl
from jax.experimental.pallas import tpu as pltpu
from jax.sharding import PartitionSpec as P

LIGHT_DEPTH = 1.5
VIEW_DEPTH = 2.0
LANES = 128
SUB = 8
SHIFTS = (-1, 0, 1)
MESH = pl.DeviceIdType.MESH


def chunked(plane):
    return jnp.stack([plane[:, k : k + LANES] for k in range(0, plane.shape[1], LANES)])


def slide(planes, amount, fill):
    if amount == 0:
        return planes
    count = planes.shape[0]
    whole, part = divmod(abs(amount), LANES)
    whole = min(whole, count)
    lane = lax.broadcasted_iota(jnp.int32, planes.shape, 2)

    def blocks(n):
        return [jnp.full((n,) + planes.shape[1:], fill, planes.dtype)] if n else []

    if amount > 0:
        if whole:
            planes = jnp.concatenate(blocks(whole) + [planes[: count - whole]] * (whole < count), axis=0)
        if part:
            turned = pltpu.roll(planes, part, 2)
            before = jnp.concatenate(blocks(1) + [turned[:-1]], axis=0)
            planes = jnp.where(lane < part, before, turned)
    else:
        if whole:
            planes = jnp.concatenate([planes[whole:]] * (whole < count) + blocks(whole), axis=0)
        if part:
            turned = pltpu.roll(planes, LANES - part, 2)
            after = jnp.concatenate([turned[1:]] + blocks(1), axis=0)
            planes = jnp.where(lane >= LANES - part, after, turned)
    return planes


def column_sums(planes):
    for bit in (1, 2, 4):
        pairs = planes.reshape(planes.shape[0] // 2, 2, SUB, LANES)
        even, odd = pairs[:, 0], pairs[:, 1]
        row = lax.broadcasted_iota(jnp.int32, even.shape, 1)
        first = (row & bit) == 0
        planes = jnp.where(first, even, odd) + pltpu.roll(jnp.where(first, odd, even), SUB - bit, 1)
    return planes.reshape(planes.shape[0] * SUB, LANES)


def kernel(
    light_count, view_count, density_hbm, albedo_hbm, color_hbm, shift_hbm, flip_hbm, out_ref,
    density, albedo, color, lateral, flips, ahead_of, tinted, totals, entered, received,
    part, part_total, swap, swap_total, comb, comb_total, got, got_total, rows4,
    load_sem, exit_send, exit_recv, core_send, core_recv, z_send, z_recv,
):
    slices, cells, columns = density.shape
    lights = color.shape[1]
    z_count = view_count // 2
    stages = light_count.bit_length() - 1
    chunks = columns // LANES
    rows = got.shape[3]
    per_slice = chunks // rows
    light_step = LIGHT_DEPTH / (slices * light_count)
    view_step = VIEW_DEPTH / (cells * view_count)

    loads = [
        pltpu.make_async_copy(density_hbm.at[x], density.at[x], load_sem.at[x]) for x in range(slices)
    ] + [
        pltpu.make_async_copy(src, dst, load_sem.at[slices + i])
        for i, (src, dst) in enumerate(
            ((flip_hbm, flips), (albedo_hbm, albedo), (shift_hbm, lateral), (color_hbm, color))
        )
    ]
    for load in loads:
        load.start()

    me_light = lax.axis_index("light")
    me_view = lax.axis_index("view")
    core = lax.rem(me_view, 2)
    z = lax.div(me_view, 2)
    other = 1 - core

    def partner(b):
        bit = lax.rem(lax.div(me_light, 2**b), 2)
        return me_light + (1 - 2 * bit) * 2**b

    barrier = pltpu.get_barrier_semaphore()
    for b in range(stages):
        pl.semaphore_signal(barrier, inc=1, device_id=(partner(b), me_view), device_id_type=MESH)
    pl.semaphore_signal(barrier, inc=1, device_id=(me_light, z * 2 + other), device_id_type=MESH)
    for step in range(1, z_count):
        pl.semaphore_signal(barrier, inc=1, device_id=(me_light, lax.rem(z + step, z_count) * 2 + core), device_id_type=MESH)

    ones = jnp.ones((chunks, cells, LANES), jnp.float32)
    chain = [ones] * 3
    for x in range(slices):
        loads[x].wait()
        ext = jnp.exp(-chunked(density[x]) * light_step)
        for a, amount in enumerate(SHIFTS):
            ahead_of[a, x] = chain[a]
            chain[a] = slide(chain[a] * ext, amount, 1.0)
    for a in range(3):
        totals[a, 0] = chain[a]
        entered[a] = ones

    pl.semaphore_wait(barrier, stages + 1 + z_count - 1)

    def facts(b):
        bit = lax.rem(lax.div(me_light, 2**b), 2)
        upward = lax.div(me_light, 2 ** (b + 1)) != light_count // 2 ** (b + 1) - 1
        return bit, upward

    def exit_copy(a, b):
        return pltpu.make_async_remote_copy(
            src_ref=totals.at[a, b], dst_ref=received.at[a, b],
            send_sem=exit_send.at[a, b], recv_sem=exit_recv.at[a, b],
            device_id=(partner(b), me_view), device_id_type=MESH,
        )

    def send_exit(a, b):
        bit, upward = facts(b)

        @pl.when((bit == 0) | upward)
        def _():
            exit_copy(a, b).start()

    def advance(a, b):
        amount = SHIFTS[a]
        bit, upward = facts(b)

        @pl.when((bit == 1) | upward)
        def _():
            exit_copy(a, b).wait_recv()

        @pl.when(bit == 1)
        def _():
            moved = received[a, b]
            for k in range(b):
                inner = lax.rem(lax.div(me_light, 2**k), 2)
                moved = jnp.where(inner == 1, slide(moved, amount * slices * 2**k, 1.0), moved)
            entered[a] = moved * entered[a]

        if b + 1 < stages:

            @pl.when(upward)
            def _():
                mine, theirs = totals[a, b], received[a, b]
                lower = jnp.where(bit == 1, theirs, mine)
                upper = jnp.where(bit == 1, mine, theirs)
                totals[a, b + 1] = slide(lower, amount * slices * 2**b, 1.0) * upper

            send_exit(a, b + 1)

    for a in range(3):
        send_exit(a, 0)

    loads[slices].wait()
    loads[slices + 1].wait()
    cell = lax.broadcasted_iota(jnp.int32, (chunks, cells, LANES), 1)
    for x in range(slices):
        depth = chunked(density[x]) * view_step
        running = depth
        for step in (1, 2, 4):
            running = running + jnp.where(cell >= step, pltpu.roll(running, step, 1), 0.0)
        column = jnp.broadcast_to(running[:, cells - 1 :, :], running.shape)
        ahead = jnp.where(flips[x] == 1, column - running, running - depth)
        weight = jnp.exp(-ahead) * (1.0 - jnp.exp(-depth))
        for c in range(3):
            tinted[c, x] = weight * chunked(albedo[c, x].astype(jnp.float32))
        total = column_sums(depth)
        for j in range(per_slice):
            piece = x * per_slice + j
            part_total[piece % 2, piece // 2] = total[j * rows : (j + 1) * rows]

    def core_copy(src, dst, index):
        return pltpu.make_async_remote_copy(
            src_ref=src, dst_ref=dst, send_sem=core_send.at[index], recv_sem=core_recv.at[index],
            device_id=(me_light, z * 2 + other), device_id_type=MESH,
        )

    total_swap = core_copy(part_total.at[other], swap_total, 3)
    total_swap.start()

    def z_copy(src, dst, index, step):
        return pltpu.make_async_remote_copy(
            src_ref=src, dst_ref=dst, send_sem=z_send.at[index, step], recv_sem=z_recv.at[index, z],
            device_id=(me_light, lax.rem(z + step, z_count) * 2 + core), device_id_type=MESH,
        )

    def z_wait(dst, index, step):
        source = lax.rem(z + step, z_count)
        pltpu.make_async_remote_copy(
            src_ref=dst.at[source], dst_ref=dst.at[source], send_sem=z_send.at[index, step],
            recv_sem=z_recv.at[index, source], device_id=(me_light, source * 2 + core), device_id_type=MESH,
        ).wait_recv()

    def flip_of(piece):
        return flips[lax.div(piece, per_slice)]

    sends = []
    swaps = []

    def share_totals():
        total_swap.wait_recv()
        comb_total[...] = part_total[core] + swap_total[...]
        for step in range(1, z_count):
            copy = z_copy(comb_total.at[lax.rem(z + step, z_count)], got_total.at[z], 3, step)
            copy.start()
            sends.append(copy)
        got_total[z] = comb_total[z]
        for target in range(z_count):
            mine_first = flip_of(target * 2 + core) == core
            mine, theirs = part_total[core, target], swap_total[target]
            part_total[core, target] = jnp.where(mine_first, 1.0, jnp.exp(-theirs))
            swap_total[target] = jnp.where(mine_first, jnp.exp(-mine), 1.0)

    def march(a):
        entering = entered[a]
        for x in range(slices):
            trans = slide(entering, SHIFTS[a] * x, 1.0) * ahead_of[a, x]
            for c in range(3):
                sums = column_sums(trans * tinted[c, x])
                for j in range(per_slice):
                    piece = x * per_slice + j
                    part[a, piece % 2, piece // 2, c] = sums[j * rows : (j + 1) * rows]
        copy = core_copy(part.at[a, other], swap.at[a], a)
        copy.start()
        swaps.append(copy)

    def finish_swap(a):
        swaps[a].wait_recv()
        for target in range(z_count):
            mine_fade, their_fade = part_total[core, target], swap_total[target]
            for c in range(3):
                comb[a, target, c] = mine_fade * part[a, core, target, c] + their_fade * swap[a, target, c]
        for step in range(1, z_count):
            copy = z_copy(comb.at[a, lax.rem(z + step, z_count)], got.at[a, z], a, step)
            copy.start()
            sends.append(copy)
        got[a, z] = comb[a, z]

    for wave in range(stages + 2):
        for a in range(2, -1, -1):
            b = wave - a
            if 0 <= b < stages:
                advance(a, b)
            if wave == 0 and a == 0:
                share_totals()
            if b == stages - 1:
                march(a)
                if a > 0:
                    finish_swap(a - 1)
    finish_swap(2)

    loads[slices + 2].wait()
    loads[slices + 3].wait()
    for step in range(1, z_count):
        z_wait(got_total, 3, step)
    flip = flip_of(me_view)
    before = jnp.zeros(got_total.shape[1:], jnp.float32)
    fades = []
    for source in range(z_count):
        fades.append(before)
        before = before + got_total[source]
    for source in range(z_count):
        depth = jnp.where(flip == 1, before - fades[source] - got_total[source], fades[source])
        fades[source] = jnp.exp(-depth)
    opacity = 1.0 - jnp.exp(-before)
    for a in range(3):
        for step in range(1, z_count):
            z_wait(got.at[a], a, step)
        for c in range(3):
            value = fades[0] * got[a, 0, c]
            for source in range(1, z_count):
                value = value + fades[source] * got[a, source, c]
            rows4[a, pl.ds(c, rows, stride=4), :] = value
        rows4[a, pl.ds(3, rows, stride=4), :] = opacity
    field = lax.rem(lax.broadcasted_iota(jnp.int32, rows4.shape[1:], 0), 4)
    for light in range(lights):
        step = lateral[light]
        picked = jnp.where(step == SHIFTS[2], rows4[2], jnp.where(step == SHIFTS[0], rows4[0], rows4[1]))
        tint = jnp.where(
            field == 0, color[0, light], jnp.where(field == 1, color[1, light], jnp.where(field == 2, color[2, light], 1.0))
        )
        lit = picked * tint
        for r in range(rows):
            out_ref[light, :, r * LANES : (r + 1) * LANES] = lit[r * 4 : (r + 1) * 4, :]

    for copy in sends:
        copy.wait_send()
    for copy in swaps:
        copy.wait_send()
    total_swap.wait_send()
    for b in range(stages):
        bit, upward = facts(b)

        @pl.when((bit == 0) | upward)
        def _():
            for a in range(3):
                exit_copy(a, b).wait_send()


def local(density, albedo, light_color, light_shift, view_flip):
    slices, cells, columns = density.shape
    lights = light_shift.shape[0]
    light_count = lax.axis_size("light")
    view_count = lax.axis_size("view")
    z_count = view_count // 2
    stages = light_count.bit_length() - 1
    chunks = columns // LANES
    piece = slices * columns // view_count
    rows = piece // LANES
    f32 = jnp.float32
    anywhere = pl.BlockSpec(memory_space=pl.ANY)
    dma = pltpu.SemaphoreType.DMA
    return pl.pallas_call(
        functools.partial(kernel, light_count, view_count),
        out_shape=jax.ShapeDtypeStruct((lights, 4, piece), f32),
        in_specs=[anywhere] * 5,
        out_specs=pl.BlockSpec(memory_space=pltpu.VMEM),
        scratch_shapes=[
            pltpu.VMEM(density.shape, f32),
            pltpu.VMEM(albedo.shape, albedo.dtype),
            pltpu.SMEM((3, lights), f32),
            pltpu.SMEM((lights,), jnp.int32),
            pltpu.SMEM((slices,), jnp.int32),
            pltpu.VMEM((3, slices, chunks, cells, LANES), f32),
            pltpu.VMEM((3, slices, chunks, cells, LANES), f32),
            pltpu.VMEM((3, stages, chunks, cells, LANES), f32),
            pltpu.VMEM((3, chunks, cells, LANES), f32),
            pltpu.VMEM((3, stages, chunks, cells, LANES), f32),
            pltpu.VMEM((3, 2, z_count, 3, rows, LANES), f32),
            pltpu.VMEM((2, z_count, rows, LANES), f32),
            pltpu.VMEM((3, z_count, 3, rows, LANES), f32),
            pltpu.VMEM((z_count, rows, LANES), f32),
            pltpu.VMEM((3, z_count, 3, rows, LANES), f32),
            pltpu.VMEM((z_count, rows, LANES), f32),
            pltpu.VMEM((3, z_count, 3, rows, LANES), f32),
            pltpu.VMEM((z_count, rows, LANES), f32),
            pltpu.VMEM((3, rows * 4, LANES), f32),
            dma((slices + 4,)),
            dma((3, stages)),
            dma((3, stages)),
            dma((4,)),
            dma((4,)),
            dma((4, z_count)),
            dma((4, z_count)),
        ],
        compiler_params=pltpu.CompilerParams(
            collective_id=0, has_side_effects=True, vmem_limit_bytes=56 * 2**20
        ),
    )(density, albedo, light_color.T, light_shift, view_flip)


def solution(mesh):
    return jax.shard_map(
        local,
        mesh=mesh,
        in_specs=(P("light", "view", None), P(None, "light", "view", None), P(), P(), P("light")),
        out_specs=P(None, None, ("light", "view")),
        check_vma=False,
    )
```

time: 27.7 us -> 23.7 us (0.86)
  local copies, waits for them, and re-layouts: 3.6 us -> 1.67 us
  other arithmetic: 1.57 us -> 0 us
  Pallas kernels: 22.2 us -> 21.8 us
    unnamed x9 -> x1, local copies, waits for them, and re-layouts: 3.58 us -> 1.67 us
    mul x1 -> x0, other arithmetic: 0.91 us -> none  [local(): return picked * tint[:, :, None]]
    eq x1 -> x0, other arithmetic: 0.66 us -> none  [local(): lateral == 1]
    pallas_call x1, Pallas kernels: 22.2 us -> 21.8 us  [local(): pl.pallas_call(functools.partial(kernel, light_count, view_count), out_sh...]
where the time goes in v2:
time: 23.7 us; the launch traced here: 23.5 us
  Pallas kernels  21.8 us (92%)
  local copies, waits for them, and re-layouts  1.67 us (7%)
    pallas_call x1, Pallas kernels, local(): pl.pallas_call(functools.partial(kernel, light_count, view_count), out_sh...  21.8 us
    unnamed x1, local copies, waits for them, and re-layouts  1.67 us

profile of v2, /device:TPU:5, one launch (start us, length us, event | category | flops | bytes accessed | tf_op | source)
XLA Modules:
  0.0 23.5 jit_solution(16935565336890353537)
XLA Ops:
  0.0 21.8 %shard_map.55 = f32[8,4,2048]{2,1,0:T(4,128)} custom-call(f32[8,8,2048]{2,1,0:T(8,128)} %density_hbm.1, bf16[3,8,8,2048]{3,2,1,0:T(8,128)(2,1)} %albedo_hbm.1, f32[3,8]{1,0:T(4,128)} %bitcast.1, s32[8]{0:T(128)} %shift_hbm.1, s32[8]{0:T(128)} %flip_hbm.1), custom_call_target="tpu_custom_call" | custom-call | tf_op jit(solution)/shard_map/pallas_call | solution.py:325
  21.8 1.7 %copy.7 = f32[8,4,2048]{2,1,0:T(4,128)} copy(f32[8,4,2048]{2,1,0:T(4,128)} %shard_map.55) | data formatting | bytes 524288

commit v3 on v2

--- a/solution.py
+++ b/solution.py
@@ -57,10 +57,11 @@
 
 
 def kernel(
-    light_count, view_count, density_hbm, albedo_hbm, color_hbm, shift_hbm, flip_hbm, out_ref,
+    light_count, view_count, density_hbm, albedo_hbm, color_hbm, shift_hbm, flip_hbm,
+    out0, out1, out2, tint0, tint1, tint2,
     density, albedo, color, lateral, flips, ahead_of, tinted, totals, entered, received,
-    part, part_total, swap, swap_total, comb, comb_total, got, got_total, rows4,
-    load_sem, exit_send, exit_recv, core_send, core_recv, z_send, z_recv,
+    part, part_total, swap, swap_total, comb, comb_total, got, got_total, rows4, planes, tints,
+    load_sem, store_sem, exit_send, exit_recv, core_send, core_recv, z_send, z_recv,
 ):
     slices, cells, columns = density.shape
     lights = color.shape[1]
@@ -160,9 +161,14 @@
 
             send_exit(a, b + 1)
 
-    for a in range(3):
-        send_exit(a, 0)
-
+    def drain_exit(a):
+        bit, upward = facts(0)
+
+        @pl.when((bit == 0) | upward)
+        def _():
+            exit_copy(a, 0).wait_send()
+
+    send_exit(0, 0)
     loads[slices].wait()
     loads[slices + 1].wait()
     cell = lax.broadcasted_iota(jnp.int32, (chunks, cells, LANES), 1)
@@ -180,6 +186,10 @@
         for j in range(per_slice):
             piece = x * per_slice + j
             part_total[piece % 2, piece // 2] = total[j * rows : (j + 1) * rows]
+        for a in (1, 2):
+            if x + 1 == a * slices // 3:
+                drain_exit(a - 1)
+                send_exit(a, 0)
 
     def core_copy(src, dst, index):
         return pltpu.make_async_remote_copy(
@@ -205,6 +215,21 @@
 
     def flip_of(piece):
         return flips[lax.div(piece, per_slice)]
+
+    loads[slices + 2].wait()
+    loads[slices + 3].wait()
+    lane = lax.broadcasted_iota(jnp.int32, tints.shape[1:], 1)
+    for light in range(lights):
+        red, green, blue = (color[c, light] for c in range(3))
+        tint = jnp.where(lane == 0, red, jnp.where(lane == 1, green, jnp.where(lane == 2, blue, 1.0)))
+        step = lateral[light]
+        for a, amount in enumerate(SHIFTS):
+            tints[a, light : light + 1, :] = jnp.where(step == amount, tint, 0.0)[light : light + 1]
+    stores = []
+    for a, target in enumerate((tint0, tint1, tint2)):
+        store = pltpu.make_async_copy(tints.at[a], target, store_sem.at[3 + a])
+        store.start()
+        stores.append(store)
 
     sends = []
     swaps = []
@@ -261,8 +286,6 @@
                     finish_swap(a - 1)
     finish_swap(2)
 
-    loads[slices + 2].wait()
-    loads[slices + 3].wait()
     for step in range(1, z_count):
         z_wait(got_total, 3, step)
     flip = flip_of(me_view)
@@ -284,17 +307,14 @@
                 value = value + fades[source] * got[a, source, c]
             rows4[a, pl.ds(c, rows, stride=4), :] = value
         rows4[a, pl.ds(3, rows, stride=4), :] = opacity
-    field = lax.rem(lax.broadcasted_iota(jnp.int32, rows4.shape[1:], 0), 4)
-    for light in range(lights):
-        step = lateral[light]
-        picked = jnp.where(step == SHIFTS[2], rows4[2], jnp.where(step == SHIFTS[0], rows4[0], rows4[1]))
-        tint = jnp.where(
-            field == 0, color[0, light], jnp.where(field == 1, color[1, light], jnp.where(field == 2, color[2, light], 1.0))
-        )
-        lit = picked * tint
         for r in range(rows):
-            out_ref[light, :, r * LANES : (r + 1) * LANES] = lit[r * 4 : (r + 1) * 4, :]
-
+            planes[a, :, r * LANES : (r + 1) * LANES] = rows4[a, r * 4 : (r + 1) * 4, :]
+        store = pltpu.make_async_copy(planes.at[a], (out0, out1, out2)[a], store_sem.at[a])
+        store.start()
+        stores.append(store)
+
+    for store in stores:
+        store.wait()
     for copy in sends:
         copy.wait_send()
     for copy in swaps:
@@ -305,7 +325,7 @@
 
         @pl.when((bit == 0) | upward)
         def _():
-            for a in range(3):
+            for a in range(2 if b == 0 else 0, 3):
                 exit_copy(a, b).wait_send()
 
 
@@ -322,11 +342,14 @@
     f32 = jnp.float32
     anywhere = pl.BlockSpec(memory_space=pl.ANY)
     dma = pltpu.SemaphoreType.DMA
-    return pl.pallas_call(
+    outs = pl.pallas_call(
         functools.partial(kernel, light_count, view_count),
-        out_shape=jax.ShapeDtypeStruct((lights, 4, piece), f32),
+        out_shape=(
+            *[jax.ShapeDtypeStruct((4, piece), f32)] * 3,
+            *[jax.ShapeDtypeStruct((lights, 4), f32)] * 3,
+        ),
         in_specs=[anywhere] * 5,
-        out_specs=pl.BlockSpec(memory_space=pltpu.VMEM),
+        out_specs=[anywhere] * 6,
         scratch_shapes=[
             pltpu.VMEM(density.shape, f32),
             pltpu.VMEM(albedo.shape, albedo.dtype),
@@ -347,7 +370,10 @@
             pltpu.VMEM((3, z_count, 3, rows, LANES), f32),
             pltpu.VMEM((z_count, rows, LANES), f32),
             pltpu.VMEM((3, rows * 4, LANES), f32),
+            pltpu.VMEM((3, 4, piece), f32),
+            pltpu.VMEM((3, lights, 4), f32),
             dma((slices + 4,)),
+            dma((6,)),
             dma((3, stages)),
             dma((3, stages)),
             dma((4,)),
@@ -359,6 +385,11 @@
             collective_id=0, has_side_effects=True, vmem_limit_bytes=56 * 2**20
         ),
     )(density, albedo, light_color.T, light_shift, view_flip)
+    planes, tints = outs[:3], outs[3:]
+    image = tints[0][:, :, None] * planes[0][None]
+    for a in range(1, 3):
+        image = image + tints[a][:, :, None] * planes[a][None]
+    return image
 
 
 def solution(mesh):

time: 23.7 us -> 25.2 us (1.063)
  the two profiles are of different devices: /device:TPU:5 before, /device:TPU:4 now
where the time goes in v3:
time: 25.2 us; the launch traced here: 25 us
  Pallas kernels  22.6 us (90%)
  other arithmetic  1.66 us (7%)
  local copies, waits for them, and re-layouts  0.68 us (3%)
    pallas_call x1, Pallas kernels, local(): pl.pallas_call(functools.partial(kernel, light_count, view_count), out_sh...  22.6 us
    add x1, other arithmetic, local(): image = image + tints[a][:, :, None] * planes[a][None]  1.66 us
    unnamed x4, local copies, waits for them, and re-layouts  0.68 us

profile of v3, /device:TPU:4, one launch (start us, length us, event | category | flops | bytes accessed | tf_op | source)
XLA Modules:
  0.0 25.0 jit_solution(18044587428814612566)
XLA Ops:
  0.0 22.6 %shard_map.55 = (f32[4,2048]{1,0:T(4,128)}, f32[4,2048]{1,0:T(4,128)}, f32[4,2048]{1,0:T(4,128)}, f32[8,4]{1,0:T(8,128)}, f32[8,4]{1,0:T(8,128)}, /*index=5*/f32[8,4]{1,0:T(8,128)}) custom-call(f32[8,8,2048]{2,1,0:T(8,128)} %density_hbm.1, bf16[3,8,8,2048]{3,2,1,0:T(8,128)(2,1)} %albedo_hbm.1, f32[3,8]{1,0:T(4,128)} %bitcast.1, s32[8]{0:T(128)} %shift_hbm.1, ...), custom_call_target="tpu_custom_call" | custom-call | tf_op jit(solution)/shard_map/pallas_call | solution.py:345
  22.6 0.0 copy-start.1
  22.7 0.0 copy-start
  22.7 0.7 %copy-done.1 = f32[8,4]{1,0:T(8,128)S(1)} copy-done((f32[8,4]{1,0:T(8,128)S(1)}, f32[8,4]{1,0:T(8,128)}, u32[]{:S(2)}) %copy-start.1) | copy-done | bytes 152
  23.3 0.0 copy-done
  23.3 1.7 %multiply_add_fusion = f32[8,4,2048]{2,1,0:T(4,128)} fusion(f32[4,2048]{1,0:T(4,128)} %get-tuple-element.16, f32[8,4]{1,0:T(8,128)} %get-tuple-element.15, f32[4,2048]{1,0:T(4,128)} %get-tuple-element.14, f32[8,4]{1,0:T(8,128)S(1)} %copy-done.1, f32[4,2048]{1,0:T(4,128)} %get-tuple-element.12, f32[8,4]{1,0:T(8,128)S(1)} %copy-done), kind=kLoop, calls=%fused_computation | loop fusion | flops 327680 | bytes 360832 | tf_op jit(solution)/shard_map/add | solution.py:391
Async XLA Ops:
  22.6 0.7 %copy-start.1 = (f32[8,4]{1,0:T(8,128)S(1)}, f32[8,4]{1,0:T(8,128)}, u32[]{:S(2)}) copy-start(f32[8,4]{1,0:T(8,128)} %get-tuple-element.13) | copy-start | bytes 388
  22.7 0.7 %copy-start = (f32[8,4]{1,0:T(8,128)S(1)}, f32[8,4]{1,0:T(8,128)}, u32[]{:S(2)}) copy-start(f32[8,4]{1,0:T(8,128)} %get-tuple-element.11) | copy-start | bytes 388

commit v4 on v2

--- a/solution.py
+++ b/solution.py
@@ -58,7 +58,7 @@
 
 def kernel(
     light_count, view_count, density_hbm, albedo_hbm, color_hbm, shift_hbm, flip_hbm, out_ref,
-    density, albedo, color, lateral, flips, ahead_of, tinted, totals, entered, received,
+    density, albedo, color, lateral, flips, ahead_of, tinted, totals, entered, received, cross_in, cross_out,
     part, part_total, swap, swap_total, comb, comb_total, got, got_total, rows4,
     load_sem, exit_send, exit_recv, core_send, core_recv, z_send, z_recv,
 ):
@@ -121,10 +121,62 @@
 
     def exit_copy(a, b):
         return pltpu.make_async_remote_copy(
-            src_ref=totals.at[a, b], dst_ref=received.at[a, b],
+            src_ref=totals.at[a, b, low], dst_ref=received.at[a, b, low],
             send_sem=exit_send.at[a, b], recv_sem=exit_recv.at[a, b],
             device_id=(partner(b), me_view), device_id_type=MESH,
         )
+
+    half = chunks // 2
+    crossed = stages == 2 and chunks % 2 == 0 and 3 * slices <= LANES
+    reach = half + 1 if crossed else chunks
+    low = pl.ds(0, reach)
+    high = pl.ds(chunks - reach, reach)
+
+    def cross_copy(a, b):
+        return pltpu.make_async_remote_copy(
+            src_ref=totals.at[a, 0, high] if b == 0 else cross_out.at[a], dst_ref=cross_in.at[a, b],
+            send_sem=exit_send.at[a, stages + b], recv_sem=exit_recv.at[a, stages + b],
+            device_id=(partner(1 - b), me_view), device_id_type=MESH,
+        )
+
+    def cross_first(a):
+        @pl.when(me_light < 2)
+        def _():
+            cross_copy(a, 0).start()
+
+        @pl.when(me_light == 0)
+        def _():
+            cross_out[a] = totals[a, 0, high]
+            cross_copy(a, 1).start()
+
+    def cross_second(a):
+        @pl.when(me_light >= 2)
+        def _():
+            cross_copy(a, 0).wait_recv()
+            came = cross_in[a, 0]
+            joined = slide(came, SHIFTS[a] * slices * 2, 1.0) * totals[a, 0, high]
+            cross_out[a] = jnp.where(me_light == 2, joined, came)
+            cross_copy(a, 1).start()
+
+    def cross_end(a):
+        @pl.when(me_light >= 1)
+        def _():
+            cross_copy(a, 1).wait_recv()
+            entered[a, half:] = cross_in[a, 1, 1:]
+
+        @pl.when(me_light >= 2)
+        def _():
+            moved = slide(cross_in[a, 0], SHIFTS[a] * slices, 1.0) * cross_in[a, 1]
+            entered[a, half:] = moved[1:]
+
+    def cross_drain(a):
+        @pl.when(me_light < 2)
+        def _():
+            cross_copy(a, 0).wait_send()
+
+        @pl.when(me_light != 1)
+        def _():
+            cross_copy(a, 1).wait_send()
 
     def send_exit(a, b):
         bit, upward = facts(b)
@@ -143,25 +195,27 @@
 
         @pl.when(bit == 1)
         def _():
-            moved = received[a, b]
+            moved = received[a, b, low]
             for k in range(b):
                 inner = lax.rem(lax.div(me_light, 2**k), 2)
                 moved = jnp.where(inner == 1, slide(moved, amount * slices * 2**k, 1.0), moved)
-            entered[a] = moved * entered[a]
+            entered[a, low] = moved * entered[a, low]
 
         if b + 1 < stages:
 
             @pl.when(upward)
             def _():
-                mine, theirs = totals[a, b], received[a, b]
+                mine, theirs = totals[a, b, low], received[a, b, low]
                 lower = jnp.where(bit == 1, theirs, mine)
                 upper = jnp.where(bit == 1, mine, theirs)
-                totals[a, b + 1] = slide(lower, amount * slices * 2**b, 1.0) * upper
+                totals[a, b + 1, low] = slide(lower, amount * slices * 2**b, 1.0) * upper
 
             send_exit(a, b + 1)
 
     for a in range(3):
         send_exit(a, 0)
+        if crossed:
+            cross_first(a)
 
     loads[slices].wait()
     loads[slices + 1].wait()
@@ -248,17 +302,20 @@
             sends.append(copy)
         got[a, z] = comb[a, z]
 
-    for wave in range(stages + 2):
-        for a in range(2, -1, -1):
-            b = wave - a
-            if 0 <= b < stages:
-                advance(a, b)
-            if wave == 0 and a == 0:
-                share_totals()
-            if b == stages - 1:
-                march(a)
-                if a > 0:
-                    finish_swap(a - 1)
+    for b in range(stages - 1):
+        for a in range(3):
+            advance(a, b)
+            if crossed:
+                cross_second(a)
+    share_totals()
+    for a in range(3):
+        if stages:
+            advance(a, stages - 1)
+        if crossed:
+            cross_end(a)
+        march(a)
+        if a > 0:
+            finish_swap(a - 1)
     finish_swap(2)
 
     loads[slices + 2].wait()
@@ -307,6 +364,9 @@
         def _():
             for a in range(3):
                 exit_copy(a, b).wait_send()
+    if crossed:
+        for a in range(3):
+            cross_drain(a)
 
 
 def local(density, albedo, light_color, light_shift, view_flip):
@@ -338,6 +398,8 @@
             pltpu.VMEM((3, stages, chunks, cells, LANES), f32),
             pltpu.VMEM((3, chunks, cells, LANES), f32),
             pltpu.VMEM((3, stages, chunks, cells, LANES), f32),
+            pltpu.VMEM((3, 2, chunks // 2 + 1, cells, LANES), f32),
+            pltpu.VMEM((3, chunks // 2 + 1, cells, LANES), f32),
             pltpu.VMEM((3, 2, z_count, 3, rows, LANES), f32),
             pltpu.VMEM((2, z_count, rows, LANES), f32),
             pltpu.VMEM((3, z_count, 3, rows, LANES), f32),
@@ -348,15 +410,15 @@
             pltpu.VMEM((z_count, rows, LANES), f32),
             pltpu.VMEM((3, rows * 4, LANES), f32),
             dma((slices + 4,)),
-            dma((3, stages)),
-            dma((3, stages)),
+            dma((3, stages + 2)),
+            dma((3, stages + 2)),
             dma((4,)),
             dma((4,)),
             dma((4, z_count)),
             dma((4, z_count)),
         ],
         compiler_params=pltpu.CompilerParams(
-            collective_id=0, has_side_effects=True, vmem_limit_bytes=56 * 2**20
+            collective_id=0, has_side_effects=True, vmem_limit_bytes=53 * 2**20 + 2**19
         ),
     )(density, albedo, light_color.T, light_shift, view_flip)
 

time: 23.7 us -> 22.2 us (0.937)
  Pallas kernels: 21.8 us -> 20 us
  local copies, waits for them, and re-layouts: 1.67 us -> 2.06 us
    pallas_call x1, Pallas kernels: 21.8 us -> 20 us  [local(): pl.pallas_call(functools.partial(kernel, light_count, view_count), out_sh...]
    unnamed x1 -> x7, local copies, waits for them, and re-layouts: 1.67 us -> 2.06 us
where the time goes in v4:
time: 22.2 us; the launch traced here: 22.1 us
  Pallas kernels  20 us (90%)
  local copies, waits for them, and re-layouts  2.06 us (9%)
    pallas_call x1, Pallas kernels, local(): pl.pallas_call(functools.partial(kernel, light_count, view_count), out_sh...  20 us
    unnamed x7, local copies, waits for them, and re-layouts  2.06 us

profile of v4, /device:TPU:5, one launch (start us, length us, event | category | flops | bytes accessed | tf_op | source)
XLA Modules:
  0.0 22.1 jit_solution(8392220532051795300)
XLA Ops:
  0.0 0.0 copy-start.2
  0.0 0.0 copy-start.1
  0.0 0.7 %copy-done.2 = s32[8]{0:T(128)S(1)} copy-done((s32[8]{0:T(128)S(1)}, s32[8]{0:T(128)}, u32[]{:S(2)}) %copy-start.2) | copy-done | bytes 56
  0.7 0.0 copy-done.1
  0.7 0.0 copy-start
  0.7 0.7 %copy-done = f32[8,3]{0,1:T(4,128)S(1)} copy-done((f32[8,3]{0,1:T(4,128)S(1)}, f32[8,3]{0,1:T(4,128)}, u32[]{:S(2)}) %copy-start) | copy-done | bytes 120
  1.4 20.0 %shard_map.55 = f32[8,4,2048]{2,1,0:T(4,128)S(1)} custom-call(f32[8,8,2048]{2,1,0:T(8,128)} %density_hbm.1, bf16[3,8,8,2048]{3,2,1,0:T(8,128)(2,1)} %albedo_hbm.1, f32[3,8]{1,0:T(4,128)S(1)} %bitcast.1, s32[8]{0:T(128)S(1)} %copy-done.1, s32[8]{0:T(128)S(1)} %copy-done.2), custom_call_target="tpu_custom_call" | custom-call | tf_op jit(solution)/shard_map/pallas_call | solution.py:385
  21.4 0.7 %copy.7 = f32[8,4,2048]{2,1,0:T(4,128)} copy(f32[8,4,2048]{2,1,0:T(4,128)S(1)} %shard_map.55) | data formatting | bytes 524288
Async XLA Ops:
  0.0 0.7 %copy-start.2 = (s32[8]{0:T(128)S(1)}, s32[8]{0:T(128)}, u32[]{:S(2)}) copy-start(s32[8]{0:T(128)} %flip_hbm.1) | copy-start | bytes 100
  0.0 0.7 %copy-start.1 = (s32[8]{0:T(128)S(1)}, s32[8]{0:T(128)}, u32[]{:S(2)}) copy-start(s32[8]{0:T(128)} %shift_hbm.1) | copy-start | bytes 100
  0.7 0.7 %copy-start = (f32[8,3]{0,1:T(4,128)S(1)}, f32[8,3]{0,1:T(4,128)}, u32[]{:S(2)}) copy-start(f32[8,3]{0,1:T(4,128)} %param.7) | copy-start | bytes 292

commit v5 on v4

--- a/solution.py
+++ b/solution.py
@@ -418,9 +418,9 @@
             dma((4, z_count)),
         ],
         compiler_params=pltpu.CompilerParams(
-            collective_id=0, has_side_effects=True, vmem_limit_bytes=53 * 2**20 + 2**19
+            collective_id=0, has_side_effects=True, vmem_limit_bytes=32 * 2**20
         ),
-    )(density, albedo, light_color.T, light_shift, view_flip)
+    )(*(pltpu.with_memory_space_constraint(x, pltpu.HBM) for x in (density, albedo, light_color.T, light_shift, view_flip)))
 
 
 def solution(mesh):

time: 22.2 us -> 20.9 us (0.941)
  local copies, waits for them, and re-layouts: 2.06 us -> 0.71 us
    unnamed x7 -> x1, local copies, waits for them, and re-layouts: 2.06 us -> 0.71 us
where the time goes in v5:
time: 20.9 us; the launch traced here: 20.7 us
  Pallas kernels  20 us (96%)
  local copies, waits for them, and re-layouts  0.71 us (3%)
    pallas_call x1, Pallas kernels, local(): pl.pallas_call(functools.partial(kernel, light_count, view_count), out_sh...  20 us
    unnamed x1, local copies, waits for them, and re-layouts  0.71 us

profile of v5, /device:TPU:5, one launch (start us, length us, event | category | flops | bytes accessed | tf_op | source)
XLA Modules:
  0.0 20.7 jit_solution(18100105416904454447)
XLA Ops:
  0.0 20.0 %shard_map.55 = f32[8,4,2048]{2,1,0:T(4,128)S(1)} custom-call(f32[8,8,2048]{2,1,0:T(8,128)} %density_hbm.1, bf16[3,8,8,2048]{3,2,1,0:T(8,128)(2,1)} %albedo_hbm.1, f32[3,8]{1,0:T(4,128)} %bitcast.1, s32[8]{0:T(128)} %shift_hbm.1, s32[8]{0:T(128)} %flip_hbm.1), custom_call_target="tpu_custom_call" | custom-call | tf_op jit(solution)/shard_map/pallas_call | solution.py:385
  20.0 0.7 %copy.7 = f32[8,4,2048]{2,1,0:T(4,128)} copy(f32[8,4,2048]{2,1,0:T(4,128)S(1)} %shard_map.55) | data formatting | bytes 524288

commit v6 on v5

--- a/solution.py
+++ b/solution.py
@@ -59,8 +59,8 @@
 def kernel(
     light_count, view_count, density_hbm, albedo_hbm, color_hbm, shift_hbm, flip_hbm, out_ref,
     density, albedo, color, lateral, flips, ahead_of, tinted, totals, entered, received, cross_in, cross_out,
-    part, part_total, swap, swap_total, comb, comb_total, got, got_total, rows4,
-    load_sem, exit_send, exit_recv, core_send, core_recv, z_send, z_recv,
+    part, part_total, swap, swap_total, comb, comb_total, got, got_total, rows4, relay_in, relay_out,
+    load_sem, relay_recv, exit_send, exit_recv, core_send, core_recv, z_send, z_recv,
 ):
     slices, cells, columns = density.shape
     lights = color.shape[1]
@@ -257,6 +257,84 @@
             recv_sem=z_recv.at[index, source], device_id=(me_light, source * 2 + core), device_id_type=MESH,
         ).wait_recv()
 
+    relayed = z_count >= 4
+
+    def far(step):
+        if not relayed or step not in (1, z_count - 1):
+            return False
+        return z == (0 if step == z_count - 1 else z_count - 1)
+
+    def late(step):
+        if not relayed or step not in (2, z_count - 2):
+            return False
+        from_low = (z == 1) if step == z_count - 2 else False
+        from_high = (z == z_count - 2) if step == 2 else False
+        return from_low | from_high
+
+    def relay_copy(src, index, step):
+        return pltpu.make_async_remote_copy(
+            src_ref=src, dst_ref=relay_in.at[3, 0] if index == 3 else relay_in.at[index], send_sem=z_send.at[index, step], recv_sem=relay_recv.at[index],
+            device_id=(me_light, (z + 1 - 2 * lax.div(z, z_count - 1)) * 2 + core), device_id_type=MESH,
+        )
+
+    def spread(pieces, dst, index):
+        for step in range(1, z_count):
+            target = lax.rem(z + step, z_count)
+            copy = z_copy(pieces.at[target], dst.at[z], index, step)
+            is_far, is_late = far(step), late(step)
+            if is_far is False and is_late is False:
+                copy.start()
+            else:
+                if is_far is not False:
+
+                    @pl.when(is_far)
+                    def _():
+                        relay_copy(pieces.at[target], index, step).start()
+
+                @pl.when(jnp.logical_not(is_far | is_late))
+                def _():
+                    copy.start()
+
+            sends.append(copy)
+
+    def relay(index):
+        if not relayed:
+            return
+        for step in sorted({2, z_count - 2}):
+
+            @pl.when(late(step))
+            def _():
+                target = lax.rem(z + step, z_count)
+                relay_copy(relay_in.at[3, 0] if index == 3 else relay_in.at[index], index, step).wait_recv()
+                if index == 3:
+                    theirs, mine = relay_in[3, 0], comb_total[target]
+                    relay_out[3, 0] = mine + theirs
+                    mine_first = flip_of(target * 2 + core) == (z == 1).astype(jnp.int32)
+                    relay_out[3, 1] = jnp.where(mine_first, 1.0, jnp.exp(-theirs))
+                    relay_out[3, 2] = jnp.where(mine_first, jnp.exp(-mine), 1.0)
+                    z_copy(relay_out.at[3, 0], got_total.at[z], 3, step).start()
+                else:
+                    for c in range(3):
+                        relay_out[index, c] = (
+                            relay_out[3, 1] * comb[index, target, c] + relay_out[3, 2] * relay_in[index, c]
+                        )
+                    z_copy(relay_out.at[index], got.at[index, z], index, step).start()
+
+    def z_arrive(dst, index, step):
+        is_far = far(step)
+        if is_far is False:
+            z_wait(dst, index, step)
+        else:
+
+            @pl.when(jnp.logical_not(is_far))
+            def _():
+                z_wait(dst, index, step)
+
+            @pl.when(is_far)
+            def _():
+                source = lax.rem(z + step, z_count)
+                dst[source] = jnp.zeros(dst.shape[1:], jnp.float32)
+
     def flip_of(piece):
         return flips[lax.div(piece, per_slice)]
 
@@ -266,10 +344,7 @@
     def share_totals():
         total_swap.wait_recv()
         comb_total[...] = part_total[core] + swap_total[...]
-        for step in range(1, z_count):
-            copy = z_copy(comb_total.at[lax.rem(z + step, z_count)], got_total.at[z], 3, step)
-            copy.start()
-            sends.append(copy)
+        spread(comb_total, got_total, 3)
         got_total[z] = comb_total[z]
         for target in range(z_count):
             mine_first = flip_of(target * 2 + core) == core
@@ -296,10 +371,7 @@
             mine_fade, their_fade = part_total[core, target], swap_total[target]
             for c in range(3):
                 comb[a, target, c] = mine_fade * part[a, core, target, c] + their_fade * swap[a, target, c]
-        for step in range(1, z_count):
-            copy = z_copy(comb.at[a, lax.rem(z + step, z_count)], got.at[a, z], a, step)
-            copy.start()
-            sends.append(copy)
+        spread(comb.at[a], got.at[a], a)
         got[a, z] = comb[a, z]
 
     for b in range(stages - 1):
@@ -314,14 +386,20 @@
         if crossed:
             cross_end(a)
         march(a)
-        if a > 0:
+        if a == 0:
+            relay(3)
+        else:
             finish_swap(a - 1)
+        if a > 1:
+            relay(a - 2)
     finish_swap(2)
+    relay(1)
+    relay(2)
 
     loads[slices + 2].wait()
     loads[slices + 3].wait()
     for step in range(1, z_count):
-        z_wait(got_total, 3, step)
+        z_arrive(got_total, 3, step)
     flip = flip_of(me_view)
     before = jnp.zeros(got_total.shape[1:], jnp.float32)
     fades = []
@@ -334,7 +412,7 @@
     opacity = 1.0 - jnp.exp(-before)
     for a in range(3):
         for step in range(1, z_count):
-            z_wait(got.at[a], a, step)
+            z_arrive(got.at[a], a, step)
         for c in range(3):
             value = fades[0] * got[a, 0, c]
             for source in range(1, z_count):
@@ -409,7 +487,10 @@
             pltpu.VMEM((3, z_count, 3, rows, LANES), f32),
             pltpu.VMEM((z_count, rows, LANES), f32),
             pltpu.VMEM((3, rows * 4, LANES), f32),
+            pltpu.VMEM((4, 3, rows, LANES), f32),
+            pltpu.VMEM((4, 3, rows, LANES), f32),
             dma((slices + 4,)),
+            dma((4,)),
             dma((3, stages + 2)),
             dma((3, stages + 2)),
             dma((4,)),

time: 20.9 us -> 21.9 us (1.048)
  the two profiles are of different devices: /device:TPU:5 before, /device:TPU:4 now
where the time goes in v6:
time: 21.9 us; the launch traced here: 21.7 us
  Pallas kernels  21 us (96%)
  local copies, waits for them, and re-layouts  0.71 us (3%)
    pallas_call x1, Pallas kernels, local(): pl.pallas_call(functools.partial(kernel, light_count, view_count), out_sh...  21 us
    unnamed x1, local copies, waits for them, and re-layouts  0.71 us

profile of v6, /device:TPU:4, one launch (start us, length us, event | category | flops | bytes accessed | tf_op | source)
XLA Modules:
  0.0 21.7 jit_solution(14016525294429275165)
XLA Ops:
  0.0 21.0 %shard_map.55 = f32[8,4,2048]{2,1,0:T(4,128)S(1)} custom-call(f32[8,8,2048]{2,1,0:T(8,128)} %density_hbm.1, bf16[3,8,8,2048]{3,2,1,0:T(8,128)(2,1)} %albedo_hbm.1, f32[3,8]{1,0:T(4,128)} %bitcast.1, s32[8]{0:T(128)} %shift_hbm.1, s32[8]{0:T(128)} %flip_hbm.1), custom_call_target="tpu_custom_call" | custom-call | tf_op jit(solution)/shard_map/pallas_call | solution.py:463
  21.0 0.7 %copy.7 = f32[8,4,2048]{2,1,0:T(4,128)} copy(f32[8,4,2048]{2,1,0:T(4,128)S(1)} %shard_map.55) | data formatting | bytes 524288

commit v7 on v5

--- a/solution.py
+++ b/solution.py
@@ -277,18 +277,35 @@
             part_total[core, target] = jnp.where(mine_first, 1.0, jnp.exp(-theirs))
             swap_total[target] = jnp.where(mine_first, jnp.exp(-mine), 1.0)
 
-    def march(a):
+    def render(a, wanted):
         entering = entered[a]
-        for x in range(slices):
+        for x in wanted:
             trans = slide(entering, SHIFTS[a] * x, 1.0) * ahead_of[a, x]
             for c in range(3):
                 sums = column_sums(trans * tinted[c, x])
                 for j in range(per_slice):
                     piece = x * per_slice + j
                     part[a, piece % 2, piece // 2, c] = sums[j * rows : (j + 1) * rows]
+
+    def render_half(a, own):
+        for parity in range(2):
+
+            @pl.when((core if own else other) == parity)
+            def _():
+                render(a, range(parity, slices, 2))
+
+    def march(a):
+        if per_slice == 1:
+            render_half(a, False)
+        else:
+            render(a, range(slices))
         copy = core_copy(part.at[a, other], swap.at[a], a)
         copy.start()
         swaps.append(copy)
+        if a > 0:
+            finish_swap(a - 1)
+        if per_slice == 1:
+            render_half(a, True)
 
     def finish_swap(a):
         swaps[a].wait_recv()
@@ -314,8 +331,6 @@
         if crossed:
             cross_end(a)
         march(a)
-        if a > 0:
-            finish_swap(a - 1)
     finish_swap(2)
 
     loads[slices + 2].wait()

time: 20.9 us -> 20.8 us (level)
  no operation moved by 1% of the time
where the time goes in v7:
time: 20.8 us; the launch traced here: 20.6 us
  Pallas kernels  19.9 us (96%)
  local copies, waits for them, and re-layouts  0.71 us (3%)
    pallas_call x1, Pallas kernels, local(): pl.pallas_call(functools.partial(kernel, light_count, view_count), out_sh...  19.9 us
    unnamed x1, local copies, waits for them, and re-layouts  0.71 us

profile of v7, /device:TPU:5, one launch (start us, length us, event | category | flops | bytes accessed | tf_op | source)
XLA Modules:
  0.0 20.6 jit_solution(7446696666389620557)
XLA Ops:
  0.0 19.9 %shard_map.55 = f32[8,4,2048]{2,1,0:T(4,128)S(1)} custom-call(f32[8,8,2048]{2,1,0:T(8,128)} %density_hbm.1, bf16[3,8,8,2048]{3,2,1,0:T(8,128)(2,1)} %albedo_hbm.1, f32[3,8]{1,0:T(4,128)} %bitcast.1, s32[8]{0:T(128)} %shift_hbm.1, s32[8]{0:T(128)} %flip_hbm.1), custom_call_target="tpu_custom_call" | custom-call | tf_op jit(solution)/shard_map/pallas_call | solution.py:400
  19.9 0.7 %copy.7 = f32[8,4,2048]{2,1,0:T(4,128)} copy(f32[8,4,2048]{2,1,0:T(4,128)S(1)} %shard_map.55) | data formatting | bytes 524288

commit v8 on v7

--- a/solution.py
+++ b/solution.py
@@ -216,6 +216,12 @@
         send_exit(a, 0)
         if crossed:
             cross_first(a)
+
+    def forward(a):
+        for b in range(stages - 1):
+            advance(a, b)
+        if crossed:
+            cross_second(a)
 
     loads[slices].wait()
     loads[slices + 1].wait()
@@ -234,6 +240,9 @@
         for j in range(per_slice):
             piece = x * per_slice + j
             part_total[piece % 2, piece // 2] = total[j * rows : (j + 1) * rows]
+        for a in range(3):
+            if x + 1 == slices - (2 - a) * slices // 4:
+                forward(a)
 
     def core_copy(src, dst, index):
         return pltpu.make_async_remote_copy(
@@ -319,11 +328,6 @@
             sends.append(copy)
         got[a, z] = comb[a, z]
 
-    for b in range(stages - 1):
-        for a in range(3):
-            advance(a, b)
-            if crossed:
-                cross_second(a)
     share_totals()
     for a in range(3):
         if stages:

time: 20.8 us -> 21.1 us (1.014)
  the two profiles are of different devices: /device:TPU:5 before, /device:TPU:0 now
where the time goes in v8:
time: 21.1 us; the launch traced here: 21 us
  Pallas kernels  20.3 us (96%)
  local copies, waits for them, and re-layouts  0.71 us (3%)
    pallas_call x1, Pallas kernels, local(): pl.pallas_call(functools.partial(kernel, light_count, view_count), out_sh...  20.3 us
    unnamed x1, local copies, waits for them, and re-layouts  0.71 us

profile of v8, /device:TPU:0, one launch (start us, length us, event | category | flops | bytes accessed | tf_op | source)
XLA Modules:
  0.0 21.0 jit_solution(7803482478672273579)
XLA Ops:
  0.0 20.3 %shard_map.55 = f32[8,4,2048]{2,1,0:T(4,128)S(1)} custom-call(f32[8,8,2048]{2,1,0:T(8,128)} %density_hbm.1, bf16[3,8,8,2048]{3,2,1,0:T(8,128)(2,1)} %albedo_hbm.1, f32[3,8]{1,0:T(4,128)} %bitcast.1, s32[8]{0:T(128)} %shift_hbm.1, s32[8]{0:T(128)} %flip_hbm.1), custom_call_target="tpu_custom_call" | custom-call | tf_op jit(solution)/shard_map/pallas_call | solution.py:404
  20.3 0.7 %copy.7 = f32[8,4,2048]{2,1,0:T(4,128)} copy(f32[8,4,2048]{2,1,0:T(4,128)S(1)} %shard_map.55) | data formatting | bytes 524288

commit v9 on v5

--- a/solution.py
+++ b/solution.py
@@ -144,12 +144,12 @@
         def _():
             cross_copy(a, 0).start()
 
+    def cross_second(a):
         @pl.when(me_light == 0)
         def _():
             cross_out[a] = totals[a, 0, high]
             cross_copy(a, 1).start()
 
-    def cross_second(a):
         @pl.when(me_light >= 2)
         def _():
             cross_copy(a, 0).wait_recv()

time: 20.9 us -> 20.8 us (level)
  no operation moved by 1% of the time
where the time goes in v9:
time: 20.8 us; the launch traced here: 20.7 us
  Pallas kernels  20 us (96%)
  local copies, waits for them, and re-layouts  0.71 us (3%)
    pallas_call x1, Pallas kernels, local(): pl.pallas_call(functools.partial(kernel, light_count, view_count), out_sh...  20 us
    unnamed x1, local copies, waits for them, and re-layouts  0.71 us

profile of v9, /device:TPU:5, one launch (start us, length us, event | category | flops | bytes accessed | tf_op | source)
XLA Modules:
  0.0 20.7 jit_solution(14742909401355056281)
XLA Ops:
  0.0 20.0 %shard_map.55 = f32[8,4,2048]{2,1,0:T(4,128)S(1)} custom-call(f32[8,8,2048]{2,1,0:T(8,128)} %density_hbm.1, bf16[3,8,8,2048]{3,2,1,0:T(8,128)(2,1)} %albedo_hbm.1, f32[3,8]{1,0:T(4,128)} %bitcast.1, s32[8]{0:T(128)} %shift_hbm.1, s32[8]{0:T(128)} %flip_hbm.1), custom_call_target="tpu_custom_call" | custom-call | tf_op jit(solution)/shard_map/pallas_call | solution.py:385
  20.0 0.7 %copy.7 = f32[8,4,2048]{2,1,0:T(4,128)} copy(f32[8,4,2048]{2,1,0:T(4,128)S(1)} %shard_map.55) | data formatting | bytes 524288
